TPU v7x, 512 devices: a whole 4x8x8 slice. The times are simulated.
512 devices in a mesh: tm: 16 (over y, core), space: 32 (over x, z).
Axes of the slice: x: 4, y: 8, z: 8, core: 2. Of those that a mesh axis runs over, the one named last changes fastest.
Arguments:
- initial: float32 [16, 128, 32768], P('tm', None, 'space'), may hold values from -324 to 324
- rhs: float32 [16, 128, 32768], P('tm', None, 'space'), may hold values from -324 to 324
- coef: float32 [32768], P('space'), may hold values from 0.5 to 4
- stiffness: float32 [128, 128], replicated, may hold values from -0.5 to 0.5
- block_inverse: float32 [128, 128], replicated, may hold values from -0.5 to 0.5
- face_proj: float32 [192, 128], replicated, may hold values from -0.5 to 0.5
- lift: float32 [128, 192], replicated, may hold values from -0.4375 to 0.4375
- time_lift: float32 [128, 64], replicated, may hold values from -0.75 to 0.75
- neighbour: int32 [6, 32768], P(None, 'space'), may hold values from 0 to 6399, as said below
- boundary: int32 [6, 32768], P(None, 'space'), may hold values from 0 to 1, as said below
- send_list: int32 [8192], P('space'), may hold values from 0 to 2047, as said below
Outputs:
- smoothed: float32 [16, 128, 32768], P('tm', None, 'space')
- indicator: float32 [16, 32768], P('tm', 'space')
- estimate: float32 [1], replicated
Inputs may be any that keep to these rules, and one draw needn't show every extreme that they name: `neighbour`: the elements form a structured hexahedral grid numbered in a random order inside each partition; partition p holds 8 element layers and meets partitions p - 1 and p + 1 across 128 faces each, listed in the same order on both sides. Interior faces point to the opposite face of the neighbouring element; faces toward another partition point to columns 6144 and above; boundary faces may point anywhere. `boundary`: marks the outer faces of the whole grid. `send_list`: the first 128 entries of a partition list its faces facing the lower partition, the next 128 those facing the upper one, as columns of its own pool below 2048.
All inputs are finite; a program needn't handle non-finite values.
Results may differ from a plain program's by a relative error of at most 0.000059.
Values sent between devices are 32-bit elements; how exact they have to be, the bound alone decides.
A program may use at most 64 MiB of HBM per device.

v0:
```python
import jax
import jax.numpy as jnp
from jax import lax
from jax.sharding import Mesh
from jax.sharding import PartitionSpec as P

SPACE = ("space_0", "space_1")
TM = ("tm_0", "tm_1")


def padded(x, sides, width):
    for axis, dim in sides:
        devices, length = (lax.axis_size(axis), x.shape[dim])
        up = [(i, (i + 1) % devices) for i in range(devices - 1)]
        down = [(j, i) for i, j in up]
        last = lax.slice_in_dim(x, length - width, length, axis=dim)
        initial = lax.slice_in_dim(x, 0, width, axis=dim)
        before = lax.ppermute(last, axis, up)
        after = lax.ppermute(initial, axis, down)
        x = jnp.concatenate([before, x, after], axis=dim)
    return x


def shifted(value, axis, steps):
    count = lax.axis_size(axis)
    initial, last = (max(0, -steps), min(count, count - steps))
    return lax.ppermute(value, axis, [(source, source + steps) for source in range(initial, last)])


def from_everyone(x, axis):
    devices = lax.axis_size(axis)
    return lax.all_to_all(jnp.broadcast_to(x[None], (devices, *x.shape)), axis, 0, 0, tiled=True)


def of_everyone(x, axis):
    return from_everyone(x, axis).sum(axis=0)


def one_axis_at_a_time(x, axes):
    far, near = axes
    return of_everyone(of_everyone(x, near), far)


def in_one(arrays, axis):
    vector, at, done = (jnp.concatenate([a.reshape(-1) for a in arrays]), 0, [])
    total = one_axis_at_a_time(vector, axis)
    for a in arrays:
        done.append(total[at : at + a.size].reshape(a.shape))
        at += a.size
    return tuple(done)


def on_device(
    initial,
    rhs,
    coef,
    stiffness,
    block_inverse,
    face_proj,
    lift,
    time_lift,
    neighbour,
    boundary,
    send_list,
):
    start_field = initial[0]
    source = rhs[0]
    elements = start_field.shape[1]
    half_dofs = start_field.shape[0] // 2
    face_dofs = face_proj.shape[0] // 6
    border = send_list.shape[0] // 2
    column_ids = neighbour.reshape(6 * elements)
    open_faces = jnp.tile(1.0 - boundary.astype(jnp.float32), (face_dofs, 1))

    def operate(vector):
        traces = jnp.dot(face_proj, vector, precision=lax.Precision.HIGHEST)
        trace_pool = traces.reshape(face_dofs, 6 * elements)
        outbound = jnp.take(trace_pool, send_list, axis=1)
        received = padded(outbound, ((SPACE, 1),), border)
        from_lower = received[:, :border]
        from_upper = received[:, 3 * border :]
        prev_end = shifted(vector[half_dofs:], TM, 1)
        ext_pool = jnp.concatenate([trace_pool, from_lower, from_upper], axis=1)
        outside = jnp.take(ext_pool, column_ids, axis=1).reshape(face_dofs * 6, elements)
        face_jump = traces - outside * open_faces
        time_jump = vector[:half_dofs] - prev_end
        applied = coef * jnp.dot(stiffness, vector, precision=lax.Precision.HIGHEST)
        applied = applied + jnp.dot(lift, face_jump, precision=lax.Precision.HIGHEST)
        applied = applied + jnp.dot(time_lift, time_jump, precision=lax.Precision.HIGHEST)
        return (applied, face_jump, time_jump)

    applied_base, base_jump, base_time = operate(start_field)
    residual = source - applied_base
    direction = jnp.dot(block_inverse, residual, precision=lax.Precision.HIGHEST) / coef
    image, step_jump, step_time = operate(direction)
    cross_sum = jnp.sum(residual * image)
    image_sum = jnp.sum(image * image)
    base_sum = (
        jnp.sum(residual * residual)
        + 0.5 * jnp.sum(base_jump * base_jump)
        + jnp.sum(base_time * base_time)
    )
    mixed_sum = 0.5 * jnp.sum(base_jump * step_jump) + jnp.sum(base_time * step_time)
    square_sum = 0.5 * jnp.sum(step_jump * step_jump) + jnp.sum(step_time * step_time)
    total_cross, total_image, total_base, total_mixed, total_square = in_one(
        (cross_sum, image_sum, base_sum, mixed_sum, square_sum),
        (("tm_0", "tm_1"), ("space_0", "space_1")),
    )
    step_size = total_cross / total_image
    smoothed = start_field + step_size * direction
    new_residual = residual - step_size * image
    new_jump = base_jump + step_size * step_jump
    new_time = base_time + step_size * step_time
    element_eta = (
        jnp.sum(new_residual * new_residual, axis=0)
        + 0.5 * jnp.sum(new_jump * new_jump, axis=0)
        + jnp.sum(new_time * new_time, axis=0)
    )
    eta_total = (
        total_base
        - 2.0 * step_size * total_cross
        + 2.0 * step_size * total_mixed
        + step_size * step_size * (total_image + total_square)
    )
    element_count = elements * lax.axis_size(TM) * lax.axis_size(SPACE)
    indicator = element_eta * element_count / eta_total
    estimate = jnp.sqrt(eta_total / element_count).reshape(1)
    return (smoothed[None], indicator[None], estimate)


def solution(mesh):
    torus = Mesh(mesh.devices.reshape(8, 2, 4, 8), ("tm_0", "tm_1", "space_0", "space_1"))
    return jax.shard_map(
        on_device,
        mesh=torus,
        in_specs=(
            P(TM, None, SPACE),
            P(TM, None, SPACE),
            P(SPACE),
            P(),
            P(),
            P(),
            P(),
            P(),
            P(None, SPACE),
            P(None, SPACE),
            P(SPACE),
        ),
        out_specs=(P(TM, None, SPACE), P(TM, SPACE), P()),
        check_vma=False,
    )
```

profile of v0, /device:TPU:1, one launch (start us, length us, event | category | flops | bytes accessed | tf_op | source)
XLA Modules:
  0.0 181.1 jit_solution(328556535275142488)
XLA Ops:
  2.1 1.8 %fusion.4 = f32[192,1024]{1,0:T(8,128)S(1)} fusion(f32[192,128]{1,0:T(8,128)S(1)} %copy-done, f32[1,128,1024]{2,1,0:T(8,128)} %param.15), kind=kOutput, calls=%fused_computation.27 | convolution fusion | flops 301989888 | bytes 1409024 | tf_op jit(solution)/shard_map/dot_general | solution.py:76
  6.0 2.0 %copy.51 = f32[32,6144]{0,1:T(8,128)S(1)} copy(f32[32,6144]{1,0:T(8,128)} %reshape.116) | data formatting | bytes 1572864 | tf_op jit(solution)/shard_map/reshape | solution.py:77
  9.6 4.8 %collective-permute-start = (f32[32,128]{0,1:T(8,128)}, f32[32,128]{0,1:T(8,128)S(1)}, u32[]{:S(2)}, u32[]{:S(2)}) collective-permute-start(f32[32,128]{0,1:T(8,128)} %get-tuple-element.18), channel_id=1, source_target_pairs={{0,1},{1,2},{2,3},{3,4},{4,5},{5,6},{6,7},{7,8},{8,9},{9,10},{10,1... | collective-permute-start | bytes 49160 | tf_op jit(solution)/shard_map/ppermute | solution.py:18
  17.4 4.0 %collective-permute-start.2 = (f32[64,1024]{1,0:T(8,128)}, f32[64,1024]{1,0:T(8,128)}, u32[]{:S(2)}, u32[]{:S(2)}) collective-permute-start(f32[64,1024]{1,0:T(8,128)} %slice_bitcast_fusion), channel_id=1, source_target_pairs={{0,32},{32,64},{64,96},{96,128},{128,160},{160,192},{192,224},{224... | collective-permute-start | bytes 786440 | tf_op jit(solution)/shard_map/ppermute | solution.py:27
  23.0 2.4 %convolution_multiply_fusion.1 = f32[128,1024]{1,0:T(8,128)} fusion(f32[128,128]{1,0:T(8,128)S(1)} %copy-done.18, f32[1,128,1024]{2,1,0:T(8,128)} %param.15, f32[1024]{0:T(1024)S(1)} %copy-done.20), kind=kOutput, calls=%fused_computation.18 | convolution fusion | flops 201457664 | bytes 1118208 | tf_op jit(solution)/shard_map/dot_general | solution.py:87
  26.6 2.2 %tile.10 = f32[192,1024]{1,0:T(8,128)} reshape(f32[32,6,1024]{2,1,0:T(8,128)} %tile.4) | data formatting | bytes 1572864 | tf_op jit(solution)/shard_map/tile | solution.py:73
  28.8 2.1 %pad_maximum_fusion = f32[32,6400]{0,1:T(8,128)S(1)} fusion(f32[32,128]{0,1:T(8,128)} %collective-permute-done.1, f32[32,128]{0,1:T(8,128)S(1)} %collective-permute-done, f32[32,6144]{0,1:T(8,128)} %copy-done.1), kind=kLoop, calls=%fused_computation.4 | loop fusion | flops 409600 | bytes 1638400 | tf_op jit(solution)/shard_map/concatenate | solution.py:83
  30.9 20.9 %gather_fusion.1 = f32[6144,32]{1,0:T(8,128)} fusion(f32[32,6400]{0,1:T(8,128)S(1)} %pad_maximum_fusion, s32[6144]{0:T(1024)S(1)} %fusion.8), kind=kCustom, calls=%fused_computation.1.clone | custom fusion | bytes 1597440 | tf_op jit(solution)/shard_map/jit(_take)/gather | solution.py:84
  51.8 4.7 %select_bitcast_fusion.1 = f32[32,6144]{0,1:T(8,128)S(1)} fusion(f32[6144,32]{1,0:T(8,128)} %gather_fusion.1, pred[6144]{0:T(1024)(128)(4,1)S(1)} %compare_and_fusion), kind=kLoop, calls=%fused_computation.7 | loop fusion | flops 196608 | bytes 1579008 | tf_op jit(solution)/shard_map/jit(_take)/select_n | solution.py:84
  56.5 1.9 %copy.52 = f32[32,6144]{1,0:T(8,128)} copy(f32[32,6144]{0,1:T(8,128)S(1)} %select_bitcast_fusion.1) | data formatting | bytes 1572864 | tf_op jit(solution)/shard_map/jit(_take)/select_n | solution.py:84
  69.7 2.0 %copy.54 = f32[32,6144]{0,1:T(8,128)S(1)} copy(f32[32,6144]{1,0:T(8,128)} %reshape.119) | data formatting | bytes 1572864 | tf_op jit(solution)/shard_map/reshape | solution.py:77
  72.5 4.6 %collective-permute-start.3 = (f32[32,128]{0,1:T(8,128)S(1)}, f32[32,128]{0,1:T(8,128)S(1)}, u32[]{:S(2)}, u32[]{:S(2)}) collective-permute-start(f32[32,128]{0,1:T(8,128)S(1)} %get-tuple-element.16), channel_id=1, source_target_pairs={{0,1},{1,2},{2,3},{3,4},{4,5},{5,6},{6,7},{7,8},{8,9},{9,10},{10,1... | collective-permute-start | bytes 49160 | tf_op jit(solution)/shard_map/ppermute | solution.py:18
  78.5 2.5 %convolution_multiply_fusion = f32[1024,128]{0,1:T(8,128)} fusion(f32[1024,128]{0,1:T(8,128)} %copy-done.7, f32[128,128]{1,0:T(8,128)S(1)} %copy-done.18, f32[1024]{0:T(1024)S(1)} %copy-done.20), kind=kOutput, calls=%fused_computation.14 | convolution fusion | flops 201457664 | bytes 1118208 | tf_op jit(solution)/shard_map/dot_general | solution.py:87
  82.6 2.4 %collective-permute-start.5 = (f32[64,1024]{1,0:T(8,128)}, f32[64,1024]{1,0:T(8,128)}, u32[]{:S(2)}, u32[]{:S(2)}) collective-permute-start(f32[64,1024]{1,0:T(8,128)} %slice.73), channel_id=1, source_target_pairs={{0,32},{32,64},{64,96},{96,128},{128,160},{160,192},{192,224},{224... | collective-permute-start | bytes 786440 | tf_op jit(solution)/shard_map/ppermute | solution.py:27
  85.0 2.1 %pad_maximum_fusion.1 = f32[32,6400]{0,1:T(8,128)S(1)} fusion(f32[32,128]{0,1:T(8,128)S(1)} %collective-permute-done.4, f32[32,128]{0,1:T(8,128)S(1)} %collective-permute-done.3, f32[32,6144]{0,1:T(8,128)} %copy-done.2), kind=kLoop, calls=%fused_computation.5 | loop fusion | flops 409600 | bytes 1638400 | tf_op jit(solution)/shard_map/concatenate | solution.py:83
  87.1 20.9 %gather_fusion.3 = f32[6144,32]{1,0:T(8,128)} fusion(f32[32,6400]{0,1:T(8,128)S(1)} %pad_maximum_fusion.1, s32[6144]{0:T(1024)S(1)} %fusion.8), kind=kCustom, calls=%fused_computation.3.clone | custom fusion | bytes 1597440 | tf_op jit(solution)/shard_map/jit(_take)/gather | solution.py:84
  108.0 4.7 %select_bitcast_fusion = f32[32,6144]{0,1:T(8,128)S(1)} fusion(f32[6144,32]{1,0:T(8,128)} %gather_fusion.3, pred[6144]{0:T(1024)(128)(4,1)S(1)} %compare_and_fusion), kind=kLoop, calls=%fused_computation.6 | loop fusion | flops 196608 | bytes 1579008 | tf_op jit(solution)/shard_map/jit(_take)/select_n | solution.py:84
  112.7 1.9 %copy.55 = f32[32,6144]{1,0:T(8,128)} copy(f32[32,6144]{0,1:T(8,128)S(1)} %select_bitcast_fusion) | data formatting | bytes 1572864 | tf_op jit(solution)/shard_map/jit(_take)/select_n | solution.py:84
  115.9 2.6 %multiply_reduce_fusion.1 = (f32[]{:T(128)}, f32[]{:T(128)}, f32[]{:T(128)}, f32[192,1024]{1,0:T(8,128)S(1)}) fusion(f32[192,1024]{1,0:T(8,128)} %copy-done.3, f32[192,1024]{1,0:T(8,128)} %copy-done.10, f32[192,1024]{1,0:T(8,128)S(1)} %reshape.120, f32[192,1024]{1,0:T(8,128)} %tile.10), kind=kLoop, calls=%fused_computation.21 | loop fusion | flops 1572861 | bytes 3932172 | tf_op jit(solution)/shard_map/reduce_sum | solution.py:104
  120.6 2.6 %convolution_add_fusion.1 = f32[1024,128]{0,1:T(8,128)} fusion(f32[1024,128]{0,1:T(8,128)} %convolution_multiply_fusion, f32[192,1024]{1,0:T(8,128)S(1)} %get-tuple-element.15, f32[128,192]{0,1:T(8,128)} %param.21), kind=kOutput, calls=%fused_computation.11 | convolution fusion | flops 302120960 | bytes 1933312 | tf_op jit(solution)/shard_map/dot_general | solution.py:88
  123.3 2.3 %multiply_reduce_fusion.9 = (f32[]{:T(128)}, f32[]{:T(128)}, f32[]{:T(128)}, f32[64,1024]{1,0:T(8,128)}) fusion(f32[64,1024]{1,0:T(8,128)S(1)} %copy-done.14, f32[64,1024]{1,0:T(8,128)} %collective-permute-done.5, f32[128,1024]{1,0:T(8,128)S(1)} %bitcast.69), kind=kLoop, calls=%fused_computation.38 | loop fusion | flops 458749 | bytes 1048588 | tf_op jit(solution)/shard_map/reduce_sum | solution.py:104
  126.9 3.2 %multiply_reduce_fusion.5 = (f32[]{:T(128)}, f32[]{:T(128)}, f32[]{:T(128)}, f32[128,1024]{1,0:T(8,128)}) fusion(f32[128,1024]{1,0:T(8,128)S(1)} %copy-done.12, f32[1024,128]{0,1:T(8,128)} %convolution_add_fusion.1, f32[64,1024]{1,0:T(8,128)} %get-tuple-element.14, f32[128,64]{0,1:T(8,128)S(1)} %copy-done.19), kind=kOutput, calls=%fused_computation.32 | convolution fusion | flops 101580800 | bytes 1867788 | tf_op jit(solution)/shard_map/dot_general | solution.py:89
  132.8 23.6 %all_to_all.12 = f32[32,1,5]{2,1,0:T(1,128)S(1)} all-to-all(f32[32,1,5]{2,1,0:T(1,128)S(1)} %broadcast_in_dim.24), channel_id=1, replica_groups=mesh['tm_0'=8,'tm_1'=2,'space_0'=4,'space_1'=8] {'space_0','space_1'}, dimensions={0} | all-to-all | bytes 1280 | tf_op jit(solution)/shard_map/all_to_all | solution.py:32
  156.4 14.4 %all_to_all.13 = f32[16,1,5]{2,1,0:T(1,128)S(1)} all-to-all(f32[16,1,5]{2,1,0:T(1,128)S(1)} %broadcast_in_dim.38), channel_id=1, replica_groups=mesh['tm_0'=8,'tm_1'=2,'space_0'=4,'space_1'=8] {'tm_0','tm_1'}, dimensions={0} | all-to-all | bytes 640 | tf_op jit(solution)/shard_map/all_to_all | solution.py:32
  (93 shorter events, 33.0 us)
Async XLA Ops:
  2.1 6.7 %copy-start.21 = (pred[256]{0:T(512)(128)(4,1)}, pred[256]{0:T(512)(128)(4,1)S(1)}, u32[]{:S(2)}) copy-start(pred[256]{0:T(512)(128)(4,1)S(1)} %compare_and_fusion.1) | copy-start | bytes 772
  4.8 18.2 %copy-start.18 = (f32[128,128]{1,0:T(8,128)S(1)}, f32[128,128]{1,0:T(8,128)}, u32[]{:S(2)}) copy-start(f32[128,128]{1,0:T(8,128)} %param.18) | copy-start | bytes 196612
  4.8 18.2 %copy-start.20 = (f32[1024]{0:T(1024)S(1)}, f32[1024]{0:T(1024)}, u32[]{:S(2)}) copy-start(f32[1024]{0:T(1024)} %param.17) | copy-start | bytes 12292
  8.0 20.8 %copy-start.1 = (f32[32,6144]{0,1:T(8,128)}, f32[32,6144]{0,1:T(8,128)S(1)}, u32[]{:S(2)}) copy-start(f32[32,6144]{0,1:T(8,128)S(1)} %copy.51) | copy-start | bytes 2359300
  9.6 19.2 %collective-permute-start = (f32[32,128]{0,1:T(8,128)}, f32[32,128]{0,1:T(8,128)S(1)}, u32[]{:S(2)}, u32[]{:S(2)}) collective-permute-start(f32[32,128]{0,1:T(8,128)} %get-tuple-element.18), channel_id=1, source_target_pairs={{0,1},{1,2},{2,3},{3,4},{4,5},{5,6},{6,7},{7,8},{8,9},{9,10},{10,1... | collective-permute-start | bytes 49160 | tf_op jit(solution)/shard_map/ppermute | solution.py:18
  14.4 14.3 %collective-permute-start.1 = (f32[32,128]{0,1:T(8,128)S(1)}, f32[32,128]{0,1:T(8,128)}, u32[]{:S(2)}, u32[]{:S(2)}) collective-permute-start(f32[32,128]{0,1:T(8,128)S(1)} %get-tuple-element.19), channel_id=1, source_target_pairs={{1,0},{2,1},{3,2},{4,3},{5,4},{6,5},{7,6},{8,7},{9,8},{10,9},{11,1... | collective-permute-start | bytes 49160 | tf_op jit(solution)/shard_map/ppermute | solution.py:19
  17.4 44.7 %collective-permute-start.2 = (f32[64,1024]{1,0:T(8,128)}, f32[64,1024]{1,0:T(8,128)}, u32[]{:S(2)}, u32[]{:S(2)}) collective-permute-start(f32[64,1024]{1,0:T(8,128)} %slice_bitcast_fusion), channel_id=1, source_target_pairs={{0,32},{32,64},{64,96},{96,128},{128,160},{160,192},{192,224},{224... | collective-permute-start | bytes 786440 | tf_op jit(solution)/shard_map/ppermute | solution.py:27
  58.4 3.0 %copy-start.15 = (f32[128,1024]{1,0:T(8,128)S(1)}, f32[128,1024]{1,0:T(8,128)}, u32[]{:S(2)}) copy-start(f32[128,1024]{1,0:T(8,128)} %convolution_multiply_fusion.1) | copy-start | bytes 1572868
  58.4 3.0 %copy-start.17 = (f32[128,192]{0,1:T(8,128)S(1)}, f32[128,192]{0,1:T(8,128)}, u32[]{:S(2)}) copy-start(f32[128,192]{0,1:T(8,128)} %param.21) | copy-start | bytes 294916
  58.4 3.8 %copy-start.5 = (f32[1,128,1024]{2,1,0:T(8,128)S(1)}, f32[1,128,1024]{2,1,0:T(8,128)}, u32[]{:S(2)}) copy-start(f32[1,128,1024]{2,1,0:T(8,128)} %param.15) | copy-start | bytes 1572868
  59.8 4.1 %copy-start.16 = (f32[1,128,1024]{2,1,0:T(8,128)S(1)}, f32[1,128,1024]{2,1,0:T(8,128)}, u32[]{:S(2)}) copy-start(f32[1,128,1024]{2,1,0:T(8,128)} %param.16) | copy-start | bytes 1572868
  59.8 4.1 %copy-start.19 = (f32[128,64]{0,1:T(8,128)S(1)}, f32[128,64]{0,1:T(8,128)}, u32[]{:S(2)}) copy-start(f32[128,64]{0,1:T(8,128)} %param.22) | copy-start | bytes 98308
  59.8 5.5 %copy-start.23 = (f32[128,128]{1,0:T(8,128)S(1)}, f32[128,128]{1,0:T(8,128)}, u32[]{:S(2)}) copy-start(f32[128,128]{1,0:T(8,128)} %param.19) | copy-start | bytes 196612
  61.4 4.5 %copy-start.3 = (f32[192,1024]{1,0:T(8,128)}, f32[192,1024]{1,0:T(8,128)S(1)}, u32[]{:S(2)}) copy-start(f32[192,1024]{1,0:T(8,128)S(1)} %multiply_subtract_fusion.1) | copy-start | bytes 2359300
  68.5 3.9 %copy-start.22 = (pred[256]{0:T(512)(128)(4,1)S(1)}, pred[256]{0:T(512)(128)(4,1)}, u32[]{:S(2)}) copy-start(pred[256]{0:T(512)(128)(4,1)} %copy-done.21) | copy-start | bytes 772
  71.7 13.3 %copy-start.2 = (f32[32,6144]{0,1:T(8,128)}, f32[32,6144]{0,1:T(8,128)S(1)}, u32[]{:S(2)}) copy-start(f32[32,6144]{0,1:T(8,128)S(1)} %copy.54) | copy-start | bytes 2359300
  72.5 12.4 %collective-permute-start.3 = (f32[32,128]{0,1:T(8,128)S(1)}, f32[32,128]{0,1:T(8,128)S(1)}, u32[]{:S(2)}, u32[]{:S(2)}) collective-permute-start(f32[32,128]{0,1:T(8,128)S(1)} %get-tuple-element.16), channel_id=1, source_target_pairs={{0,1},{1,2},{2,3},{3,4},{4,5},{5,6},{6,7},{7,8},{8,9},{9,10},{10,1... | collective-permute-start | bytes 49160 | tf_op jit(solution)/shard_map/ppermute | solution.py:18
  77.2 7.8 %collective-permute-start.4 = (f32[32,128]{0,1:T(8,128)S(1)}, f32[32,128]{0,1:T(8,128)S(1)}, u32[]{:S(2)}, u32[]{:S(2)}) collective-permute-start(f32[32,128]{0,1:T(8,128)S(1)} %get-tuple-element.17), channel_id=1, source_target_pairs={{1,0},{2,1},{3,2},{4,3},{5,4},{6,5},{7,6},{8,7},{9,8},{10,9},{11,1... | collective-permute-start | bytes 49160 | tf_op jit(solution)/shard_map/ppermute | solution.py:19
  82.6 40.6 %collective-permute-start.5 = (f32[64,1024]{1,0:T(8,128)}, f32[64,1024]{1,0:T(8,128)}, u32[]{:S(2)}, u32[]{:S(2)}) collective-permute-start(f32[64,1024]{1,0:T(8,128)} %slice.73), channel_id=1, source_target_pairs={{0,32},{32,64},{64,96},{96,128},{128,160},{160,192},{192,224},{224... | collective-permute-start | bytes 786440 | tf_op jit(solution)/shard_map/ppermute | solution.py:27
  115.9 7.4 %copy-start.8 = (f32[1024,128]{0,1:T(8,128)S(1)}, f32[1024,128]{0,1:T(8,128)}, u32[]{:S(2)}) copy-start(f32[1024,128]{0,1:T(8,128)} %copy-done.7) | copy-start | bytes 1572868
  115.9 7.4 %copy-start.14 = (f32[64,1024]{1,0:T(8,128)S(1)}, f32[64,1024]{1,0:T(8,128)}, u32[]{:S(2)}) copy-start(f32[64,1024]{1,0:T(8,128)} %copy-done.13) | copy-start | bytes 786436
  115.9 11.0 %copy-start.12 = (f32[128,1024]{1,0:T(8,128)S(1)}, f32[128,1024]{1,0:T(8,128)}, u32[]{:S(2)}) copy-start(f32[128,1024]{1,0:T(8,128)} %copy-done.11) | copy-start | bytes 1572868
  118.5 54.4 %copy-start.4 = (f32[192,1024]{1,0:T(8,128)S(1)}, f32[192,1024]{1,0:T(8,128)}, u32[]{:S(2)}) copy-start(f32[192,1024]{1,0:T(8,128)} %copy-done.3) | copy-start | bytes 2359300
  120.6 53.5 %copy-start.6 = (f32[1,128,1024]{2,1,0:T(8,128)S(1)}, f32[1,128,1024]{2,1,0:T(8,128)}, u32[]{:S(2)}) copy-start(f32[1,128,1024]{2,1,0:T(8,128)} %param.15) | copy-start | bytes 1572868
  (6 other events, 5.6 us)
where the time goes:
time: 182 us; the launch traced here: 181 us
  local copies, waits for them, and re-layouts  70.5 us (39%)
  blocking collectives  38 us (21%)
  other arithmetic  27.3 us (15%)
  starting transfers between devices  18.4 us (10%)
  matrix products  15.3 us (8%)
  between operations  11.4 us (6%)
    gather x2, local copies, waits for them, and re-layouts, operate(): jnp.take(ext_pool, column_ids, axis=1).reshape(face_dofs * 6, elements)  41.8 us
    all_to_all x2, blocking collectives, from_everyone(): lax.all_to_all(jnp.broadcast_to(x[None], (devices, *x.shape)), axis, 0, 0...  38 us
    ppermute x2, starting transfers between devices, padded(): before = lax.ppermute(last, axis, up)  9.44 us
    select_n x2, other arithmetic, operate(): jnp.take(ext_pool, column_ids, axis=1).reshape(face_dofs * 6, elements)  9.32 us
    ppermute x2, starting transfers between devices, shifted(): lax.ppermute(value, axis, [(source, source + steps) for source in range(i...  6.4 us
    reshape x4, local copies, waits for them, and re-layouts, operate(): trace_pool = traces.reshape(face_dofs, 6 * elements)  6.37 us
    dot_general x2, matrix products, operate(): applied = coef * jnp.dot(stiffness, vector, precision=lax.Precision.HIGHEST)  4.87 us
    concatenate x2, other arithmetic, operate(): ext_pool = jnp.concatenate([trace_pool, from_lower, from_upper], axis=1)  4.25 us
  transfers between devices with their start and end apart: 6, of which 0 were waited for; matrix products, arithmetic and copies ran while one was open for 46% of the time, Pallas kernels for 0%

commit v1 on v0

v1 whole, which is shorter than its diff:
```python
import functools

import jax
import jax.numpy as jnp
from jax import lax
from jax.experimental import pallas as pl
from jax.experimental.pallas import tpu as pltpu
from jax.sharding import PartitionSpec as P

MESH = pl.DeviceIdType.MESH
F32 = jnp.float32
BF16 = jnp.bfloat16
D = 128
H = 64
FD = 32
R = 192
LAYERS = 8
NB = 128
E = 1024


def split(x):
    high = x.astype(BF16)
    return high, (x - high.astype(F32)).astype(BF16)


def dot(a, b):
    return jnp.dot(a, b, preferred_element_type=F32)


def iota(shape, dim):
    return lax.broadcasted_iota(jnp.int32, shape, dim)


def one_hot(mask):
    return jnp.where(mask, 1.0, 0.0).astype(BF16)


def column(row):
    eye = iota((NB, NB), 0) == iota((NB, NB), 1)
    return jnp.sum(jnp.where(eye, jnp.broadcast_to(row, (NB, NB)), 0), axis=1, keepdims=True)


def lookup(table, index):
    lane = jnp.broadcast_to(index & 127, (8, NB))
    line = jnp.broadcast_to(index >> 7, (8, NB))
    found = jnp.take_along_axis(table, lane, axis=1)
    return jnp.sum(jnp.where(line == iota((8, NB), 0), found, 0), axis=0, keepdims=True)


def layer(k):
    return slice(k * NB, (k + 1) * NB)


def kernel(
    nt,
    ns,
    init_h,
    rhs_h,
    coef_h,
    stiff_h,
    binv_h,
    fproj_h,
    lift_h,
    tlift_h,
    nbr_h,
    bnd_h,
    send_h,
    out_o,
    ind_o,
    est_o,
    init_v,
    rhs_v,
    coef_v,
    stiff_v,
    binv_v,
    fproj_v,
    lift_v,
    tlift_v,
    nbr_v,
    bnd_v,
    send_v,
    place,
    x3,
    work,
    lat,
    jumps,
    jsplit,
    resid,
    direc,
    image,
    w_vol,
    w_lift,
    w_inv,
    rim_out,
    rim_in,
    end_in,
    row_a,
    row_b,
    load_sem,
    end_send,
    end_recv,
    rim_send,
    rim_recv,
    sum_send,
    sum_recv,
):
    t = lax.axis_index("tm")
    p = lax.axis_index("space")

    barrier = pltpu.get_barrier_semaphore()
    for d in range(1, nt):
        pl.semaphore_signal(barrier, inc=1, device_id={"tm": lax.rem(t + d, nt)}, device_id_type=MESH)
    for d in range(1, ns):
        pl.semaphore_signal(barrier, inc=1, device_id={"space": lax.rem(p + d, ns)}, device_id_type=MESH)

    loads = {}
    for n, (name, src, dst) in enumerate(
        (
            ("nbr", nbr_h, nbr_v),
            ("send", send_h, send_v),
            ("bnd", bnd_h, bnd_v),
            ("init", init_h.at[0], init_v),
            ("coef", coef_h, coef_v),
            ("fproj", fproj_h, fproj_v),
            ("stiff", stiff_h, stiff_v),
            ("lift", lift_h, lift_v),
            ("tlift", tlift_h, tlift_v),
            ("rhs", rhs_h.at[0], rhs_v),
            ("binv", binv_h, binv_v),
        )
    ):
        loads[name] = pltpu.make_async_copy(src, dst, load_sem.at[n])
        loads[name].start()

    loads["nbr"].wait()
    loads["send"].wait()
    loads["bnd"].wait()

    def table(ref, f):
        return jnp.concatenate([ref[f : f + 1, layer(k)] for k in range(8)], axis=0)

    first = p == 0
    lower = send_v[0:1, :] & (E - 1)
    upper = send_v[1:2, :] & (E - 1)
    chain_table = jnp.where(first, table(nbr_v, 0), table(nbr_v, 1)) & (E - 1)
    chain = [jnp.where(first, upper, lower)]
    for k in range(1, LAYERS):
        chain.append(lookup(chain_table, chain[-1]))
    slots = [jnp.where(first, chain[LAYERS - 1 - k], chain[k]) for k in range(LAYERS)]

    pl.semaphore_wait(barrier, nt + ns - 2)
    up = {"tm": lax.rem(t + 1, nt)}
    upper_part = {"space": lax.rem(p + 1, ns)}
    lower_part = {"space": lax.rem(p + ns - 1, ns)}

    def send_end(k, src):
        copy = pltpu.make_async_remote_copy(
            src_ref=src,
            dst_ref=end_in.at[k],
            send_sem=end_send.at[k],
            recv_sem=end_recv.at[k],
            device_id=up,
            device_id_type=MESH,
        )
        copy.start()
        return copy

    def send_rims(k):
        copies = []
        for side, device in ((0, upper_part), (1, lower_part)):
            copy = pltpu.make_async_remote_copy(
                src_ref=rim_out.at[k, side],
                dst_ref=rim_in.at[k, side],
                send_sem=rim_send.at[k, side],
                recv_sem=rim_recv.at[k, side],
                device_id=device,
                device_id_type=MESH,
            )
            copy.start()
            copies.append(copy)
        return copies

    loads["init"].wait()
    end_copy = send_end(0, init_v.at[pl.ds(H, H)])

    for k in range(LAYERS):
        place[:, layer(k)] = one_hot(iota((E, NB), 0) == slots[k])
    base_col = column(slots[0])
    top_col = column(slots[LAYERS - 1])
    out_map = one_hot(top_col == upper)
    in_map = one_hot(column(upper) == slots[LAYERS - 1])
    lateral = []
    for f in range(2, 6):
        target = lookup(table(nbr_v, f) & (E - 1), slots[0])
        wall = lookup(table(bnd_v, f), slots[0])
        lateral.append(one_hot((base_col == target) & (wall == 0)))
    blank = jnp.zeros((NB, NB), BF16)
    lat_maps = [
        jnp.concatenate(
            [
                jnp.concatenate([lateral[2 * g], blank], axis=1),
                jnp.concatenate([blank, lateral[2 * g + 1]], axis=1),
            ],
            axis=0,
        )
        for g in range(2)
    ]

    loads["fproj"].wait()
    loads["stiff"].wait()
    loads["lift"].wait()
    loads["tlift"].wait()
    loads["binv"].wait()
    row, col = iota((R, R), 0), iota((R, R), 1)
    to_face = one_hot(col == (row & 31) * 6 + (row >> 5))
    from_face = one_hot(row == (col & 31) * 6 + (col >> 5))
    both = dot(to_face, jnp.concatenate(split(fproj_v[...]), axis=1)).astype(BF16)
    fh, fl = both[:, :D], both[:, D:]
    sh, sl = split(stiff_v[...])
    w_vol[0:R, :] = jnp.concatenate([fh, fh, fl], axis=1)
    w_vol[R : R + D, :] = jnp.concatenate([sh, sh, sl], axis=1)
    both = dot(jnp.concatenate(split(lift_v[...]), axis=0), from_face).astype(BF16)
    th, tl = split(tlift_v[...])
    lh = jnp.concatenate([both[:D], th], axis=1)
    ll = jnp.concatenate([both[D:], tl], axis=1)
    w_lift[...] = jnp.concatenate([lh, lh, ll], axis=1)
    bh, bl = split(binv_v[...])
    w_inv[...] = jnp.concatenate([bh, bh, bl], axis=1)

    ih, il = split(init_v[...])
    loads["coef"].wait()
    coef = coef_v[...]
    ch = coef.astype(BF16)
    rest = coef - ch.astype(F32)
    cm = rest.astype(BF16)
    cl = (rest - cm.astype(F32)).astype(BF16)
    moved = dot(jnp.concatenate([ih, il, ch, cm, cl, jnp.zeros((13, E), BF16)], axis=0), place[...])
    coef = moved[2 * D : 2 * D + 1] + moved[2 * D + 1 : 2 * D + 2] + moved[2 * D + 2 : 2 * D + 3]
    xh = moved[0:D].astype(BF16)
    x3[0:D, :] = xh
    x3[D : 2 * D, :] = moved[D : 2 * D].astype(BF16)
    x3[2 * D : 3 * D, :] = xh
    start = moved[0:H] + moved[D : D + H]

    def traces_of(k):
        work[...] = dot(w_vol[...], x3[...])
        rim_out[k, 1] = work[0:FD, layer(0)]
        th, tl = split(work[FD : 2 * FD, layer(LAYERS - 1)])
        turned = dot(jnp.concatenate([th, tl], axis=0), out_map)
        rim_out[k, 0] = turned[:FD] + turned[FD:]

    def lateral_jumps(k):
        for g in range(2):
            a, b = 2 + 2 * g, 3 + 2 * g
            for x in range(LAYERS):
                for side, f in ((0, b), (1, a)):
                    th, tl = split(work[f * FD : (f + 1) * FD, layer(x)])
                    lat[x * 2 * FD : x * 2 * FD + FD, layer(side)] = th
                    lat[x * 2 * FD + FD : (x + 1) * 2 * FD, layer(side)] = tl
            seen = dot(lat[...], lat_maps[g])
            for x in range(LAYERS):
                both = seen[x * 2 * FD : x * 2 * FD + FD] + seen[x * 2 * FD + FD : (x + 1) * 2 * FD]
                for side, f in ((0, a), (1, b)):
                    jumps[k, f * FD : (f + 1) * FD, layer(x)] = work[f * FD : (f + 1) * FD, layer(x)] - both[:, layer(side)]
        for x in range(1, LAYERS):
            jumps[k, 0:FD, layer(x)] = work[0:FD, layer(x)] - work[FD : 2 * FD, layer(x - 1)]
            jumps[k, FD : 2 * FD, layer(x - 1)] = work[FD : 2 * FD, layer(x - 1)] - work[0:FD, layer(x)]

    def rim_jumps(k, copies):
        copies[0].wait_recv()
        copies[1].wait_recv()
        from_lower = jnp.where(p == 0, 0.0, rim_in[k, 0])
        jumps[k, 0:FD, layer(0)] = work[0:FD, layer(0)] - from_lower
        th, tl = split(rim_in[k, 1])
        turned = dot(jnp.concatenate([th, tl], axis=0), in_map)
        from_upper = jnp.where(p == ns - 1, 0.0, turned[:FD] + turned[FD:])
        last = layer(LAYERS - 1)
        jumps[k, FD : 2 * FD, last] = work[FD : 2 * FD, last] - from_upper

    def apply(k):
        jh, jl = split(jumps[k])
        jsplit[0:256, :] = jh
        jsplit[256:512, :] = jl
        jsplit[512:768, :] = jh
        return coef * work[R : R + D, :] + dot(w_lift[...], jsplit[...])

    traces_of(0)
    rims = send_rims(0)
    loads["rhs"].wait()
    moved = dot(jnp.concatenate(split(rhs_v[...]), axis=0), place[...])
    resid[...] = moved[:D] + moved[D:]
    lateral_jumps(0)
    rim_jumps(0, rims)
    end_copy.wait_recv()
    moved = dot(jnp.concatenate(split(end_in[0]), axis=0), place[...])
    jumps[0, R:, :] = start - jnp.where(t == 0, 0.0, moved[:H] + moved[H:])
    residual = resid[...] - apply(0)
    resid[...] = residual
    rh, rl = split(residual)
    x3[0:D, :] = rh
    x3[D : 2 * D, :] = rl
    x3[2 * D : 3 * D, :] = rh
    direction = dot(w_inv[...], x3[...]) / coef
    direc[...] = direction
    end_copy2 = send_end(1, direc.at[pl.ds(H, H)])
    dh, dl = split(direction)
    x3[0:D, :] = dh
    x3[D : 2 * D, :] = dl
    x3[2 * D : 3 * D, :] = dh

    traces_of(1)
    rims2 = send_rims(1)
    lateral_jumps(1)
    rim_jumps(1, rims2)
    end_copy2.wait_recv()
    jumps[1, R:, :] = direc[0:H, :] - jnp.where(t == 0, 0.0, end_in[1])
    image[...] = apply(1)

    def over(x):
        return jnp.sum(x, axis=0, keepdims=True)

    im, r = image[...], resid[...]
    cross = over(r * im)
    square = over(im * im)
    base = over(r * r) + 0.5 * over(jumps[0, :R] * jumps[0, :R]) + over(jumps[0, R:] * jumps[0, R:])
    mixed = over(jumps[0, :R] * jumps[1, :R]) + 2.0 * over(jumps[0, R:] * jumps[1, R:]) - 2.0 * cross
    quad = square + 0.5 * over(jumps[1, :R] * jumps[1, :R]) + over(jumps[1, R:] * jumps[1, R:])
    rows = jnp.concatenate([cross, square, base, mixed, quad, jnp.zeros((3, E), F32)], axis=0)
    folded = rows[:, layer(0)]
    for k in range(1, 8):
        folded = folded + rows[:, layer(k)]
    sums = jnp.sum(folded, axis=1, keepdims=True)
    diagonal = iota((8, NB), 0) == iota((8, NB), 1)
    message = jnp.sum(jnp.where(diagonal, sums, 0.0), axis=0, keepdims=True)

    def exchange(buf, me, count, axis, n):
        copies = []
        for d in range(1, count):
            copy = pltpu.make_async_remote_copy(
                src_ref=buf.at[me],
                dst_ref=buf.at[me],
                send_sem=sum_send.at[n],
                recv_sem=sum_recv.at[n],
                device_id={axis: lax.rem(me + d, count)},
                device_id_type=MESH,
            )
            copy.start()
        return pltpu.make_async_copy(buf.at[pl.ds(0, count - 1)], buf.at[pl.ds(0, count - 1)], sum_recv.at[n])

    row_a[t] = message
    got = exchange(row_a, t, nt, "tm", 0)
    a0, rest = split_rows(rows)
    back = lax.dot_general(
        jnp.concatenate([dh, dl, a0, rest], axis=0),
        place[...],
        (((1,), (1,)), ((), ())),
        preferred_element_type=F32,
    )
    got.wait()
    total = row_a[0]
    for d in range(1, nt):
        total = total + row_a[d]
    row_b[p] = total
    got_b = exchange(row_b, p, ns, "space", 1)
    got_b.wait()
    total = row_b[0]
    for d in range(1, ns):
        total = total + row_b[d]
    cross, square, base, mixed, quad = (total[0:1, k : k + 1] for k in range(5))
    step = cross / square
    eta_total = base + step * mixed + step * step * quad
    out_o[0] = init_v[...] + step * (back[:D] + back[D : 2 * D])
    parts = back[2 * D : 2 * D + 8] + back[2 * D + 8 : 2 * D + 16] + back[2 * D + 16 : 2 * D + 24]
    eta = parts[2:3] + step * parts[3:4] + step * step * parts[4:5]
    count = float(E * nt * ns)
    ind_o[...] = eta * count / eta_total
    est_o[...] = jnp.broadcast_to(jnp.sqrt(eta_total / count), (1, NB))

    end_copy.wait_send()
    end_copy2.wait_send()
    for copy in rims + rims2:
        copy.wait_send()
    for buf, count, n in ((row_a, nt, 0), (row_b, ns, 1)):
        sent = buf.at[pl.ds(0, count - 1)]
        pltpu.make_async_copy(sent, sent, sum_send.at[n]).wait()


def split_rows(rows):
    high, rest = rows.astype(BF16), None
    rest = rows - high.astype(F32)
    mid = rest.astype(BF16)
    low = (rest - mid.astype(F32)).astype(BF16)
    return high, jnp.concatenate([mid, low], axis=0)


def on_device(nt, ns, initial, rhs, coef, stiffness, block_inverse, face_proj, lift, time_lift, neighbour, boundary, send_list):
    vmem = pltpu.VMEM
    any_spec = pl.BlockSpec(memory_space=pl.ANY)
    vmem_spec = pl.BlockSpec(memory_space=vmem)
    smoothed, indicator, estimate = pl.pallas_call(
        functools.partial(kernel, nt, ns),
        out_shape=(
            jax.ShapeDtypeStruct((1, D, E), F32),
            jax.ShapeDtypeStruct((1, E), F32),
            jax.ShapeDtypeStruct((1, NB), F32),
        ),
        in_specs=[any_spec] * 11,
        out_specs=[vmem_spec] * 3,
        scratch_shapes=[
            vmem((D, E), F32),
            vmem((D, E), F32),
            vmem((1, E), F32),
            vmem((D, D), F32),
            vmem((D, D), F32),
            vmem((R, D), F32),
            vmem((D, R), F32),
            vmem((D, H), F32),
            vmem((6, E), jnp.int32),
            vmem((6, E), jnp.int32),
            vmem((2, NB), jnp.int32),
            vmem((E, E), BF16),
            vmem((3 * D, E), BF16),
            vmem((R + D, E), F32),
            vmem((LAYERS * 2 * FD, 2 * NB), BF16),
            vmem((2, 256, E), F32),
            vmem((768, E), BF16),
            vmem((D, E), F32),
            vmem((D, E), F32),
            vmem((D, E), F32),
            vmem((R + D, 3 * D), BF16),
            vmem((D, 768), BF16),
            vmem((D, 3 * D), BF16),
            vmem((2, 2, FD, NB), F32),
            vmem((2, 2, FD, NB), F32),
            vmem((2, H, E), F32),
            vmem((nt, 1, NB), F32),
            vmem((ns, 1, NB), F32),
            pltpu.SemaphoreType.DMA((11,)),
            pltpu.SemaphoreType.DMA((2,)),
            pltpu.SemaphoreType.DMA((2,)),
            pltpu.SemaphoreType.DMA((2, 2)),
            pltpu.SemaphoreType.DMA((2, 2)),
            pltpu.SemaphoreType.DMA((2,)),
            pltpu.SemaphoreType.DMA((2,)),
        ],
        compiler_params=pltpu.CompilerParams(collective_id=0, has_side_effects=True, vmem_limit_bytes=48 * 1024 * 1024),
        cost_estimate=pl.CostEstimate(flops=4 * 10**9, bytes_accessed=3 * 2**20, transcendentals=0),
    )(
        initial,
        rhs,
        coef.reshape(1, E),
        stiffness,
        block_inverse,
        face_proj,
        lift,
        time_lift,
        neighbour,
        boundary,
        send_list.reshape(2, NB),
    )
    return smoothed, indicator, estimate[0, :1]


def solution(mesh):
    return jax.shard_map(
        functools.partial(on_device, mesh.shape["tm"], mesh.shape["space"]),
        mesh=mesh,
        in_specs=(
            P("tm", None, "space"),
            P("tm", None, "space"),
            P("space"),
            P(),
            P(),
            P(),
            P(),
            P(),
            P(None, "space"),
            P(None, "space"),
            P("space"),
        ),
        out_specs=(P("tm", None, "space"), P("tm", "space"), P()),
        check_vma=False,
    )
```

time: 182 us -> 45.6 us (0.25)
  local copies, waits for them, and re-layouts: 70.5 us -> 5.41 us
  blocking collectives: 38 us -> 0 us
  Pallas kernels: 0 us -> 37.9 us
  other arithmetic: 27.3 us -> 0 us
  starting transfers between devices: 18.4 us -> 0 us
  matrix products: 15.3 us -> 0 us
  between operations: 11.4 us -> 1.94 us
    gather x4 -> x0, local copies, waits for them, and re-layouts: 43.3 us -> none  [the longest x2 41.8 us: operate(): jnp.take(ext_pool, column_ids, axis=1).reshape(face_dofs * 6, elements)]
    all_to_all x2 -> x0, blocking collectives: 38 us -> none  [from_everyone(): lax.all_to_all(jnp.broadcast_to(x[None], (devices, *x.shape)), axis, 0, 0...]
    pallas_call x0 -> x1, Pallas kernels: none -> 37.9 us  [on_device(): pl.pallas_call(functools.partial(kernel, nt, ns), out_shape=(jax.ShapeDty...]
    ppermute x6 -> x0, starting transfers between devices: 18.4 us -> none  [the longest x2 9.44 us: padded(): before = lax.ppermute(last, axis, up)]
    dot_general x9 -> x0, matrix products: 15.3 us -> none  [the longest x2 4.87 us: operate(): applied = coef * jnp.dot(stiffness, vector, precision=lax.Precision.HIGHEST)]
    select_n x5 -> x0, other arithmetic: 10.2 us -> none  [the longest x2 9.32 us: operate(): jnp.take(ext_pool, column_ids, axis=1).reshape(face_dofs * 6, elements)]
    reshape x7 -> x0, local copies, waits for them, and re-layouts: 9.83 us -> none  [the longest x4 6.37 us: operate(): trace_pool = traces.reshape(face_dofs, 6 * elements)]
    reduce_sum x7 -> x0, other arithmetic: 7.34 us -> none  [the longest x1 2.65 us: on_device(): jnp.sum(step_jump * step_jump)]
  transfers between devices with their start and end apart: 6 -> 0, of which waited for: 0 -> 0; matrix products, arithmetic and copies ran while one was open for 46% -> 0% of each run, Pallas kernels for 0% -> 0%
where the time goes in v1:
time: 45.6 us; the launch traced here: 45.3 us
  Pallas kernels  37.9 us (83%)
  local copies, waits for them, and re-layouts  5.41 us (12%)
  between operations  1.94 us (4%)
    pallas_call x1, Pallas kernels, on_device(): pl.pallas_call(functools.partial(kernel, nt, ns), out_shape=(jax.ShapeDty...  37.9 us
    unnamed x22, local copies, waits for them, and re-layouts  5.41 us

profile of v1, /device:TPU:1, one launch (start us, length us, event | category | flops | bytes accessed | tf_op | source)
XLA Modules:
  0.0 45.3 jit_solution(12574345326627615930)
XLA Ops:
  0.6 0.0 copy-start.5
  0.6 0.0 copy-start.6
  0.7 0.0 copy-start.7
  0.7 0.0 copy-start.8
  0.7 0.9 %copy.15.tlift_h = f32[128,64]{1,0:T(8,128)S(1)} copy(f32[128,64]{0,1:T(8,128)} %param.18) | data formatting | bytes 65536 | tf_op args[7]
  1.5 0.0 copy-start.2
  1.6 0.0 copy-start.3
  1.6 0.0 copy-start.4
  1.6 1.0 %copy.14.lift_h = f32[128,192]{1,0:T(8,128)S(1)} copy(f32[128,192]{0,1:T(8,128)} %param.17) | data formatting | bytes 196608 | tf_op args[6]
  2.6 0.0 copy-done.5
  2.6 0.0 copy-done.6
  2.6 0.0 copy-done.7
  2.7 0.0 copy-done.8
  2.7 0.0 copy-done.2
  2.7 0.0 copy-done.3
  2.7 0.0 copy-done.4
  2.7 0.0 copy-start
  2.7 1.0 %copy-done = f32[1,128,1024]{2,1,0:T(8,128)S(1)} copy-done((f32[1,128,1024]{2,1,0:T(8,128)S(1)}, f32[1,128,1024]{2,1,0:T(8,128)}, u32[]{:S(2)}) %copy-start) | copy-done | bytes 524312
  3.7 0.0 copy-start.1
  3.7 1.0 %copy-done.1 = f32[1,128,1024]{2,1,0:T(8,128)S(1)} copy-done((f32[1,128,1024]{2,1,0:T(8,128)S(1)}, f32[1,128,1024]{2,1,0:T(8,128)}, u32[]{:S(2)}) %copy-start.1) | copy-done | bytes 524312
  4.8 37.9 %shard_map.130 = (f32[1,128,1024]{2,1,0:T(8,128)S(1)}, f32[1,1024]{1,0:T(1,128)S(1)}, f32[1,128]{1,0:T(1,128)S(1)}) custom-call(f32[1,128,1024]{2,1,0:T(8,128)S(1)} %copy-done, f32[1,128,1024]{2,1,0:T(8,128)S(1)} %copy-done.1, f32[1,1024]{1,0:T(1,128)S(1)} %bitcast.4, f32[128,128]{1,0:T(8,128)S(1)} %copy-done.3, f32[128,128]{1,0:T(8,128)S(1)} %copy-done.4, ...), custom_call_target="tpu_custom_call" | custom-call | flops 4000000000 | bytes 3145728 | tf_op jit(solution)/shard_map/pallas_call | solution.py:401
  42.7 0.8 %copy.19 = f32[1,128,1024]{2,1,0:T(8,128)} copy(f32[1,128,1024]{2,1,0:T(8,128)S(1)} %get-tuple-element.12) | data formatting | bytes 1048576
  43.5 0.6 %copy.20 = f32[1,1024]{1,0:T(1,128)} copy(f32[1,1024]{1,0:T(1,128)S(1)} %get-tuple-element.13) | data formatting | bytes 8192
Async XLA Ops:
  0.6 2.0 %copy-start.5 = (s32[6,1024]{1,0:T(8,128)S(1)}, s32[6,1024]{1,0:T(8,128)}, u32[]{:S(2)}) copy-start(s32[6,1024]{1,0:T(8,128)} %nbr_h.1) | copy-start | bytes 73732
  0.6 2.0 %copy-start.6 = (s32[6,1024]{1,0:T(8,128)S(1)}, s32[6,1024]{1,0:T(8,128)}, u32[]{:S(2)}) copy-start(s32[6,1024]{1,0:T(8,128)} %bnd_h.1) | copy-start | bytes 73732
  0.7 2.0 %copy-start.7 = (f32[1024]{0:T(1024)S(1)}, f32[1024]{0:T(1024)}, u32[]{:S(2)}) copy-start(f32[1024]{0:T(1024)} %param.13) | copy-start | bytes 12292
  0.7 2.0 %copy-start.8 = (s32[256]{0:T(256)S(1)}, s32[256]{0:T(256)}, u32[]{:S(2)}) copy-start(s32[256]{0:T(256)} %param.21) | copy-start | bytes 3076
  1.5 1.1 %copy-start.2 = (f32[192,128]{1,0:T(8,128)S(1)}, f32[192,128]{1,0:T(8,128)}, u32[]{:S(2)}) copy-start(f32[192,128]{1,0:T(8,128)} %fproj_h.1) | copy-start | bytes 294916
  1.6 1.1 %copy-start.3 = (f32[128,128]{1,0:T(8,128)S(1)}, f32[128,128]{1,0:T(8,128)}, u32[]{:S(2)}) copy-start(f32[128,128]{1,0:T(8,128)} %stiff_h.1) | copy-start | bytes 196612
  1.6 1.1 %copy-start.4 = (f32[128,128]{1,0:T(8,128)S(1)}, f32[128,128]{1,0:T(8,128)}, u32[]{:S(2)}) copy-start(f32[128,128]{1,0:T(8,128)} %binv_h.1) | copy-start | bytes 196612
  2.7 1.0 %copy-start = (f32[1,128,1024]{2,1,0:T(8,128)S(1)}, f32[1,128,1024]{2,1,0:T(8,128)}, u32[]{:S(2)}) copy-start(f32[1,128,1024]{2,1,0:T(8,128)} %init_h.1) | copy-start | bytes 1572868
  3.7 1.0 %copy-start.1 = (f32[1,128,1024]{2,1,0:T(8,128)S(1)}, f32[1,128,1024]{2,1,0:T(8,128)}, u32[]{:S(2)}) copy-start(f32[1,128,1024]{2,1,0:T(8,128)} %rhs_h.1) | copy-start | bytes 1572868

commit v2 on v1

v2 whole, which is shorter than its diff:
```python
import functools

import jax
import jax.numpy as jnp
from jax import lax
from jax.experimental import pallas as pl
from jax.experimental.pallas import tpu as pltpu
from jax.sharding import PartitionSpec as P

MESH = pl.DeviceIdType.MESH
F32 = jnp.float32
BF16 = jnp.bfloat16
D = 128
H = 64
FD = 32
R = 192
LAYERS = 8
NB = 128
E = 1024


def split(x):
    high = x.astype(BF16)
    return high, (x - high.astype(F32)).astype(BF16)


def dot(a, b):
    return jnp.dot(a, b, preferred_element_type=F32)


def iota(shape, dim):
    return lax.broadcasted_iota(jnp.int32, shape, dim)


def one_hot(mask):
    return jnp.where(mask, 1.0, 0.0).astype(BF16)


def column(row):
    eye = iota((NB, NB), 0) == iota((NB, NB), 1)
    return jnp.sum(jnp.where(eye, jnp.broadcast_to(row, (NB, NB)), 0), axis=1, keepdims=True)


def lookup(table, index):
    lane = jnp.broadcast_to(index & 127, (8, NB))
    line = jnp.broadcast_to(index >> 7, (8, NB))
    found = jnp.take_along_axis(table, lane, axis=1)
    return jnp.sum(jnp.where(line == iota((8, NB), 0), found, 0), axis=0, keepdims=True)


def layer(k):
    return slice(k * NB, (k + 1) * NB)


def rounds(n):
    out, known = [], 1
    while known < n // 2:
        out.append(known)
        known *= 2
    return out


def near(n):
    return (1,) if n == 2 else (1, n - 1)


def stack3(x):
    high, low = split(x)
    return jnp.concatenate([high, low, high], axis=0)


def over(x):
    return jnp.sum(x, axis=0, keepdims=True)


PARTS = (0, 3, 1, 2)
W = 256
CUT = 768


def part(q):
    return slice(q * W, (q + 1) * W)


def kernel(
    nt,
    ns,
    init_h,
    rhs_h,
    coef_h,
    stiff_h,
    binv_h,
    fproj_h,
    lift_h,
    tlift_h,
    nbr_h,
    bnd_h,
    send_h,
    dir_o,
    eta_o,
    tot_o,
    init_v,
    rhs_v,
    coef_v,
    stiff_v,
    binv_v,
    fproj_v,
    lift_v,
    tlift_v,
    nbr_v,
    bnd_v,
    send_v,
    place,
    xs,
    x3,
    r3,
    t3,
    work,
    lat,
    jumps,
    jsplit,
    pre,
    bpre,
    moved_end,
    resid,
    direc,
    rows,
    w_vol,
    w_lift,
    w_time,
    w_inv,
    w_both,
    rim_out,
    rim_in,
    end_in,
    row_a,
    row_b,
    load_sem,
    end_send,
    end_recv,
    rim_send,
    rim_recv,
    sum_send,
    sum_recv,
    known_sem,
):
    t = lax.axis_index("tm")
    p = lax.axis_index("space")
    axes = (("tm", t, nt, 0), ("space", p, ns, len(rounds(nt))))

    barrier = pltpu.get_barrier_semaphore()
    for axis, me, n, _ in axes:
        for d in near(n):
            pl.semaphore_signal(barrier, inc=1, device_id={axis: lax.rem(me + d, n)}, device_id_type=MESH)

    def know(k):
        for axis, me, n, base in axes:
            reach = rounds(n)
            if 0 < k <= len(reach):
                pl.semaphore_wait(known_sem.at[base + k - 1], 2)
            if k < len(reach):
                for d in (reach[k], n - reach[k]):
                    pl.semaphore_signal(known_sem.at[base + k], inc=1, device_id={axis: lax.rem(me + d, n)}, device_id_type=MESH)

    loads = {}
    for n, (name, src, dst) in enumerate(
        (
            ("send", send_h, send_v),
            ("init", init_h.at[0], init_v),
            ("fproj", fproj_h, fproj_v),
            ("nbr", nbr_h, nbr_v),
            ("bnd", bnd_h, bnd_v),
            ("coef", coef_h, coef_v),
            ("stiff", stiff_h, stiff_v),
            ("lift", lift_h, lift_v),
            ("tlift", tlift_h, tlift_v),
            ("binv", binv_h, binv_v),
            ("rhs", rhs_h.at[0], rhs_v),
        )
    ):
        loads[name] = pltpu.make_async_copy(src, dst, load_sem.at[n])
        loads[name].start()

    row, col = iota((R, R), 0), iota((R, R), 1)
    to_face = one_hot(col == (row & 31) * 6 + (row >> 5))
    loads["send"].wait()
    lower = send_v[0:1, :] & (E - 1)
    upper = send_v[1:2, :] & (E - 1)
    column_ids = iota((E, NB), 0)
    ends = jnp.concatenate([one_hot(column_ids == lower), one_hot(column_ids == upper)], axis=1)
    loads["fproj"].wait()
    both = dot(to_face, jnp.concatenate(split(fproj_v[...]), axis=1)).astype(BF16)
    fh, fl = both[:, :D], both[:, D:]
    w_vol[0:R, :] = jnp.concatenate([fh, fh, fl], axis=1)

    loads["init"].wait()
    ih, il = split(init_v[...])
    xs[0:D, :] = ih
    xs[D : 2 * D, :] = il
    picked = dot(xs[0 : 2 * D, :], ends).astype(BF16)
    rim = dot(w_vol[0 : 2 * FD, :], jnp.concatenate([picked[:D], picked[D:], picked[:D]], axis=0))
    rim_out[0, 1] = rim[0:FD, 0:NB]
    rim_out[0, 0] = rim[FD : 2 * FD, NB : 2 * NB]

    loads["nbr"].wait()
    loads["bnd"].wait()

    def table(ref, f):
        return jnp.concatenate([ref[f : f + 1, layer(k)] for k in range(8)], axis=0)

    first = p == 0
    chain_table = jnp.where(first, table(nbr_v, 0), table(nbr_v, 1)) & (E - 1)
    chain = [jnp.where(first, upper, lower)]
    for k in range(1, LAYERS):
        chain.append(lookup(chain_table, chain[-1]))
    slots = [jnp.where(first, chain[LAYERS - 1 - k], chain[k]) for k in range(LAYERS)]

    pl.semaphore_wait(barrier, len(near(nt)) + len(near(ns)))
    up = {"tm": lax.rem(t + 1, nt)}
    upper_part = {"space": lax.rem(p + 1, ns)}
    lower_part = {"space": lax.rem(p + ns - 1, ns)}

    def send_end(k, n, src, columns):
        copy = pltpu.make_async_remote_copy(
            src_ref=src.at[pl.ds(H, H), columns],
            dst_ref=end_in.at[k, :, columns],
            send_sem=end_send.at[k, n],
            recv_sem=end_recv.at[k, n],
            device_id=up,
            device_id_type=MESH,
        )
        copy.start()
        return copy

    def send_rims(k):
        copies = []
        for side, device in ((0, upper_part), (1, lower_part)):
            copy = pltpu.make_async_remote_copy(
                src_ref=rim_out.at[k, side],
                dst_ref=rim_in.at[k, side],
                send_sem=rim_send.at[k, side],
                recv_sem=rim_recv.at[k, side],
                device_id=device,
                device_id_type=MESH,
            )
            copy.start()
            copies.append(copy)
        return copies

    rims = send_rims(0)
    end_copies = [send_end(0, 0, init_v, pl.ds(0, CUT)), send_end(0, 1, init_v, pl.ds(CUT, E - CUT))]
    know(0)

    for k in range(LAYERS):
        place[:, layer(k)] = one_hot(column_ids == slots[k])
    base_col = column(slots[0])
    top_col = column(slots[LAYERS - 1])
    out_map = one_hot(top_col == upper)
    in_map = one_hot(column(upper) == slots[LAYERS - 1])
    lateral = []
    for f in range(2, 6):
        target = lookup(table(nbr_v, f) & (E - 1), slots[0])
        wall = lookup(table(bnd_v, f), slots[0])
        lateral.append(one_hot((base_col == target) & (wall == 0)))
    blank = jnp.zeros((NB, NB), BF16)
    lat_maps = [
        jnp.concatenate(
            [
                jnp.concatenate([lateral[2 * g], blank], axis=1),
                jnp.concatenate([blank, lateral[2 * g + 1]], axis=1),
            ],
            axis=0,
        )
        for g in range(2)
    ]

    loads["stiff"].wait()
    sh, sl = split(stiff_v[...])
    w_vol[R : R + D, :] = jnp.concatenate([sh, sh, sl], axis=1)

    loads["coef"].wait()
    coef = coef_v[...]
    ch = coef.astype(BF16)
    rest = coef - ch.astype(F32)
    cm = rest.astype(BF16)
    cl = (rest - cm.astype(F32)).astype(BF16)
    xs[2 * D : 2 * D + 16, :] = jnp.concatenate([ch, cm, cl, jnp.zeros((13, E), BF16)], axis=0)
    moved = dot(xs[...], place[...])
    coef = moved[2 * D : 2 * D + 1] + moved[2 * D + 1 : 2 * D + 2] + moved[2 * D + 2 : 2 * D + 3]
    inverse_coef = 1.0 / coef
    xh = moved[0:D].astype(BF16)
    x3[0:D, :] = xh
    x3[D : 2 * D, :] = moved[D : 2 * D].astype(BF16)
    x3[2 * D : 3 * D, :] = xh
    start = moved[0:H] + moved[D : D + H]

    know(1)

    def wide(high, low):
        return jnp.concatenate([high, high, low], axis=0).astype(F32).T.astype(BF16)

    loads["lift"].wait()
    both = dot(to_face, jnp.concatenate(split(lift_v[...]), axis=1))
    w_lift[...] = wide(both[:, :D], both[:, D:])
    loads["tlift"].wait()
    th, tl = split(tlift_v[...])
    w_time[...] = wide(th, tl)
    loads["binv"].wait()
    bh, bl = split(binv_v[...])
    w_inv[...] = jnp.concatenate([bh, bh, bl], axis=1)
    both = lax.dot_general(
        jnp.concatenate([th, tl, th], axis=1), w_inv[...], (((1,), (1,)), ((), ())), preferred_element_type=F32
    )
    w_both[...] = wide(*split(both))

    def lateral_jumps(k):
        for g in range(2):
            a, b = 2 + 2 * g, 3 + 2 * g
            for x in range(LAYERS):
                for side, f in ((0, b), (1, a)):
                    high, low = split(work[f * FD : (f + 1) * FD, layer(x)])
                    lat[x * 2 * FD : x * 2 * FD + FD, layer(side)] = high
                    lat[x * 2 * FD + FD : (x + 1) * 2 * FD, layer(side)] = low
            seen = dot(lat[...], lat_maps[g])
            for x in range(LAYERS):
                both = seen[x * 2 * FD : x * 2 * FD + FD] + seen[x * 2 * FD + FD : (x + 1) * 2 * FD]
                for side, f in ((0, a), (1, b)):
                    jumps[k, f * FD : (f + 1) * FD, layer(x)] = work[f * FD : (f + 1) * FD, layer(x)] - both[:, layer(side)]
        for x in range(1, LAYERS):
            jumps[k, 0:FD, layer(x)] = work[0:FD, layer(x)] - work[FD : 2 * FD, layer(x - 1)]
            jumps[k, FD : 2 * FD, layer(x - 1)] = work[FD : 2 * FD, layer(x - 1)] - work[0:FD, layer(x)]

    def rim_jumps(k, copies):
        copies[0].wait_recv()
        copies[1].wait_recv()
        from_lower = jnp.where(p == 0, 0.0, rim_in[k, 0])
        jumps[k, 0:FD, layer(0)] = work[0:FD, layer(0)] - from_lower
        turned = dot(jnp.concatenate(split(rim_in[k, 1]), axis=0), in_map)
        from_upper = jnp.where(p == ns - 1, 0.0, turned[:FD] + turned[FD:])
        last = layer(LAYERS - 1)
        jumps[k, FD : 2 * FD, last] = work[FD : 2 * FD, last] - from_upper

    def apply_local(k):
        jsplit[...] = stack3(jumps[k, 0:R])
        return coef * work[R : R + D, :] + dot(w_lift[...], jsplit[...])

    work[...] = dot(w_vol[...], x3[...])
    lateral_jumps(0)
    know(2)
    loads["rhs"].wait()
    moved = dot(jnp.concatenate(split(rhs_v[...]), axis=0), place[...])
    pre[...] = moved[:D] + moved[D:]
    rim_jumps(0, rims)
    pre[...] = pre[...] - apply_local(0)
    r3[...] = stack3(pre[...])
    bpre[...] = dot(w_inv[...], r3[...]) * inverse_coef
    know(3)

    end_copies[0].wait_recv()
    moved_end[...] = dot(jnp.concatenate(split(end_in[0, :, 0:CUT]), axis=0), place[0:CUT, :])
    end_copies[1].wait_recv()
    late = jnp.concatenate(split(end_in[0, :, CUT:E]), axis=0)
    dir_copies = {}
    for q in PARTS:
        c = part(q)
        moved = moved_end[:, c] + dot(late, place[CUT:E, c])
        jump = start[:, c] - jnp.where(t == 0, 0.0, moved[:H] + moved[H:])
        jumps[0, R:, c] = jump
        t3[:, c] = stack3(jump)
        direction = bpre[:, c] - dot(w_both[...], t3[:, c]) * inverse_coef[:, c]
        direc[:, c] = direction
        dir_copies[q] = send_end(1, q, direc, pl.ds(q * W, W))
        x3[:, c] = stack3(direction)

    for q in PARTS:
        work[:, part(q)] = dot(w_vol[...], x3[:, part(q)])
        if q == 3:
            rim_out[1, 1] = work[0:FD, layer(0)]
            turned = dot(jnp.concatenate(split(work[FD : 2 * FD, layer(LAYERS - 1)]), axis=0), out_map)
            rim_out[1, 0] = turned[:FD] + turned[FD:]
            rims2 = send_rims(1)
    know(4)
    residual = pre[...] - dot(w_time[...], t3[...])
    resid[...] = residual
    rows[2:3, :] = over(residual * residual) + 0.5 * over(jumps[0, :R] * jumps[0, :R]) + over(jumps[0, R:] * jumps[0, R:])
    lateral_jumps(1)
    rim_jumps(1, rims2)
    pre[...] = apply_local(1)
    mixed = over(jumps[0, :R] * jumps[1, :R])
    quad = 0.5 * over(jumps[1, :R] * jumps[1, :R])
    folded = jnp.zeros((8, NB), F32)
    for q in PARTS:
        c = part(q)
        dir_copies[q].wait_recv()
        jump = direc[0:H, c] - jnp.where(t == 0, 0.0, end_in[1, :, c])
        image = pre[:, c] + dot(w_time[...], stack3(jump))
        cross = over(resid[:, c] * image)
        square = over(image * image)
        part_rows = jnp.concatenate(
            [
                cross,
                square,
                rows[2:3, c],
                mixed[:, c] + 2.0 * over(jumps[0, R:, c] * jump) - 2.0 * cross,
                quad[:, c] + square + over(jump * jump),
                jnp.zeros((3, W), F32),
            ],
            axis=0,
        )
        rows[:, c] = part_rows
        folded = folded + part_rows[:, :NB] + part_rows[:, NB:]
    sums = jnp.sum(folded, axis=1, keepdims=True)
    diagonal = iota((8, NB), 0) == iota((8, NB), 1)
    message = jnp.sum(jnp.where(diagonal, sums, 0.0), axis=0, keepdims=True)

    def exchange(buf, me, count, axis, n):
        for d in range(1, count):
            pltpu.make_async_remote_copy(
                src_ref=buf.at[me],
                dst_ref=buf.at[me],
                send_sem=sum_send.at[n],
                recv_sem=sum_recv.at[n],
                device_id={axis: lax.rem(me + d, count)},
                device_id_type=MESH,
            ).start()
        others = buf.at[pl.ds(0, count - 1)]
        return pltpu.make_async_copy(others, others, sum_recv.at[n])

    row_a[t] = message
    got = exchange(row_a, t, nt, "tm", 0)
    eh = rows[...].astype(BF16)
    rest = rows[...] - eh.astype(F32)
    em = rest.astype(BF16)
    el = (rest - em.astype(F32)).astype(BF16)
    back = lax.dot_general(
        jnp.concatenate([x3[0 : 2 * D, :], eh, em, el, jnp.zeros((8, E), BF16)], axis=0),
        place[...],
        (((1,), (1,)), ((), ())),
        preferred_element_type=F32,
    )
    dir_o[...] = back[:D] + back[D : 2 * D]
    eta_o[...] = back[2 * D : 2 * D + 8] + back[2 * D + 8 : 2 * D + 16] + back[2 * D + 16 : 2 * D + 24]
    got.wait()
    total = row_a[0]
    for d in range(1, nt):
        total = total + row_a[d]
    row_b[p] = total
    exchange(row_b, p, ns, "space", 1).wait()
    total = row_b[0]
    for d in range(1, ns):
        total = total + row_b[d]
    tot_o[...] = total

    for copy in end_copies + [dir_copies[q] for q in PARTS] + rims + rims2:
        copy.wait_send()
    for buf, count, n in ((row_a, nt, 0), (row_b, ns, 1)):
        sent = buf.at[pl.ds(0, count - 1)]
        pltpu.make_async_copy(sent, sent, sum_send.at[n]).wait()


def finish(count, init_v, dir_v, eta_v, tot_v, out_o, ind_o, est_o):
    cross, square, base, mixed, quad = (tot_v[0:1, k : k + 1] for k in range(5))
    step = cross / square
    eta_total = base + step * mixed + step * step * quad
    out_o[0] = init_v[0] + step * dir_v[...]
    eta = eta_v[2:3] + step * eta_v[3:4] + step * step * eta_v[4:5]
    ind_o[...] = eta * count / eta_total
    est_o[...] = jnp.broadcast_to(jnp.sqrt(eta_total / count), (1, NB))


def on_device(nt, ns, initial, rhs, coef, stiffness, block_inverse, face_proj, lift, time_lift, neighbour, boundary, send_list):
    vmem = pltpu.VMEM
    hbm_spec = pl.BlockSpec(memory_space=pltpu.HBM)
    vmem_spec = pl.BlockSpec(memory_space=vmem)
    dma = pltpu.SemaphoreType.DMA
    direction, eta, totals = pl.pallas_call(
        functools.partial(kernel, nt, ns),
        out_shape=(
            jax.ShapeDtypeStruct((D, E), F32),
            jax.ShapeDtypeStruct((8, E), F32),
            jax.ShapeDtypeStruct((1, NB), F32),
        ),
        in_specs=[hbm_spec] * 11,
        out_specs=[vmem_spec] * 3,
        scratch_shapes=[
            vmem((D, E), F32),
            vmem((D, E), F32),
            vmem((1, E), F32),
            vmem((D, D), F32),
            vmem((D, D), F32),
            vmem((R, D), F32),
            vmem((R, D), F32),
            vmem((H, D), F32),
            vmem((6, E), jnp.int32),
            vmem((6, E), jnp.int32),
            vmem((2, NB), jnp.int32),
            vmem((E, E), BF16),
            vmem((2 * D + 16, E), BF16),
            vmem((3 * D, E), BF16),
            vmem((3 * D, E), BF16),
            vmem((3 * H, E), BF16),
            vmem((R + D, E), F32),
            vmem((LAYERS * 2 * FD, 2 * NB), BF16),
            vmem((2, 256, E), F32),
            vmem((3 * R, E), BF16),
            vmem((D, E), F32),
            vmem((D, E), F32),
            vmem((2 * H, E), F32),
            vmem((D, E), F32),
            vmem((D, E), F32),
            vmem((8, E), F32),
            vmem((R + D, 3 * D), BF16),
            vmem((D, 3 * R), BF16),
            vmem((D, 3 * H), BF16),
            vmem((D, 3 * D), BF16),
            vmem((D, 3 * H), BF16),
            vmem((2, 2, FD, NB), F32),
            vmem((2, 2, FD, NB), F32),
            vmem((2, H, E), F32),
            vmem((nt, 1, NB), F32),
            vmem((ns, 1, NB), F32),
            dma((11,)),
            dma((2, 4)),
            dma((2, 4)),
            dma((2, 2)),
            dma((2, 2)),
            dma((2,)),
            dma((2,)),
            pltpu.SemaphoreType.REGULAR((max(1, len(rounds(nt)) + len(rounds(ns))),)),
        ],
        compiler_params=pltpu.CompilerParams(collective_id=0, has_side_effects=True, vmem_limit_bytes=40 * 1024 * 1024),
        cost_estimate=pl.CostEstimate(flops=4 * 10**9, bytes_accessed=3 * 2**20, transcendentals=0),
    )(
        *(
            pltpu.with_memory_space_constraint(x, pltpu.HBM)
            for x in (
                initial,
                rhs,
                coef.reshape(1, E),
                stiffness,
                block_inverse,
                face_proj,
                lift.T,
                time_lift.T,
                neighbour,
                boundary,
                send_list.reshape(2, NB),
            )
        )
    )
    smoothed, indicator, estimate = pl.pallas_call(
        functools.partial(finish, float(E * nt * ns)),
        out_shape=(
            jax.ShapeDtypeStruct((1, D, E), F32),
            jax.ShapeDtypeStruct((1, E), F32),
            jax.ShapeDtypeStruct((1, NB), F32),
        ),
        in_specs=[vmem_spec] * 4,
        out_specs=[vmem_spec] * 3,
        compiler_params=pltpu.CompilerParams(vmem_limit_bytes=8 * 1024 * 1024),
        cost_estimate=pl.CostEstimate(flops=3 * 10**5, bytes_accessed=2**20, transcendentals=0),
    )(initial, direction, eta, totals)
    return smoothed, indicator, estimate[0, :1]


def solution(mesh):
    return jax.shard_map(
        functools.partial(on_device, mesh.shape["tm"], mesh.shape["space"]),
        mesh=mesh,
        in_specs=(
            P("tm", None, "space"),
            P("tm", None, "space"),
            P("space"),
            P(),
            P(),
            P(),
            P(),
            P(),
            P(None, "space"),
            P(None, "space"),
            P("space"),
        ),
        out_specs=(P("tm", None, "space"), P("tm", "space"), P()),
        check_vma=False,
    )
```

time: 45.6 us -> 43.2 us (0.947)
  local copies, waits for them, and re-layouts: 5.41 us -> 0.01 us
  Pallas kernels: 37.9 us -> 42.4 us
  between operations: 1.94 us -> 0.66 us
    unnamed x22 -> x2, local copies, waits for them, and re-layouts: 5.41 us -> 0.01 us
    pallas_call x1, Pallas kernels: 37.9 us -> 41.3 us  [on_device(): pl.pallas_call(functools.partial(kernel, nt, ns), out_shape=(jax.ShapeDty...]
    pallas_call x0 -> x1, Pallas kernels: none -> 1.1 us  [on_device(): pl.pallas_call(functools.partial(finish, float(E * nt * ns)), out_shape=(...]
where the time goes in v2:
time: 43.2 us; the launch traced here: 43.1 us
  Pallas kernels  42.4 us (98%)
  between operations  0.66 us (2%)
    pallas_call x1, Pallas kernels, on_device(): pl.pallas_call(functools.partial(kernel, nt, ns), out_shape=(jax.ShapeDty...  41.3 us
    pallas_call x1, Pallas kernels, on_device(): pl.pallas_call(functools.partial(finish, float(E * nt * ns)), out_shape=(...  1.1 us

profile of v2, /device:TPU:1, one launch (start us, length us, event | category | flops | bytes accessed | tf_op | source)
XLA Modules:
  0.0 43.1 jit_solution(10764608872470629650)
XLA Ops:
  0.6 0.0 copy-start
  0.6 41.3 %shard_map.130 = (f32[128,1024]{1,0:T(8,128)S(1)}, f32[8,1024]{1,0:T(8,128)S(1)}, f32[1,128]{1,0:T(1,128)S(1)}) custom-call(f32[1,128,1024]{2,1,0:T(8,128)} %init_v.1, f32[1,128,1024]{2,1,0:T(8,128)} %rhs_h.1, f32[1,1024]{1,0:T(1,128)} %bitcast.8, f32[128,128]{1,0:T(8,128)} %stiff_h.1, f32[128,128]{1,0:T(8,128)} %binv_h.1, f32[192,128]{1,0:T(8,128)} %fproj_h.1, ...), custom_call_target="tpu_custom_call" | custom-call | flops 4000000000 | bytes 3145728 | tf_op jit(solution)/shard_map/pallas_call | solution.py:476
  41.9 0.0 copy-done
  42.0 1.1 %shard_map.131 = (f32[1,128,1024]{2,1,0:T(8,128)}, f32[1,1024]{1,0:T(1,128)}, f32[1,128]{1,0:T(1,128)}) custom-call(f32[1,128,1024]{2,1,0:T(8,128)S(1)} %copy-done, f32[128,1024]{1,0:T(8,128)S(1)} %get-tuple-element.9.dir_v, f32[8,1024]{1,0:T(8,128)S(1)} %get-tuple-element.10.eta_v, f32[1,128]{1,0:T(1,128)S(1)} %get-tuple-element.11.tot_v), custom_call_target="tpu_custom_call" | custom-call | flops 300000 | bytes 1048576 | tf_op jit(solution)/shard_map/pallas_call | solution.py:551
Async XLA Ops:
  0.6 41.3 %copy-start = (f32[1,128,1024]{2,1,0:T(8,128)S(1)}, f32[1,128,1024]{2,1,0:T(8,128)}, u32[]{:S(2)}) copy-start(f32[1,128,1024]{2,1,0:T(8,128)} %init_v.1) | copy-start | bytes 1572868

commit v3 on v2

--- a/solution.py
+++ b/solution.py
@@ -111,6 +111,7 @@
     bnd_v,
     send_v,
     place,
+    start_v,
     xs,
     x3,
     r3,
@@ -153,8 +154,8 @@
         for d in near(n):
             pl.semaphore_signal(barrier, inc=1, device_id={axis: lax.rem(me + d, n)}, device_id_type=MESH)
 
-    def know(k):
-        for axis, me, n, base in axes:
+    def know(k, among=(0, 1)):
+        for axis, me, n, base in (axes[i] for i in among):
             reach = rounds(n)
             if 0 < k <= len(reach):
                 pl.semaphore_wait(known_sem.at[base + k - 1], 2)
@@ -202,19 +203,6 @@
     rim_out[0, 1] = rim[0:FD, 0:NB]
     rim_out[0, 0] = rim[FD : 2 * FD, NB : 2 * NB]
 
-    loads["nbr"].wait()
-    loads["bnd"].wait()
-
-    def table(ref, f):
-        return jnp.concatenate([ref[f : f + 1, layer(k)] for k in range(8)], axis=0)
-
-    first = p == 0
-    chain_table = jnp.where(first, table(nbr_v, 0), table(nbr_v, 1)) & (E - 1)
-    chain = [jnp.where(first, upper, lower)]
-    for k in range(1, LAYERS):
-        chain.append(lookup(chain_table, chain[-1]))
-    slots = [jnp.where(first, chain[LAYERS - 1 - k], chain[k]) for k in range(LAYERS)]
-
     pl.semaphore_wait(barrier, len(near(nt)) + len(near(ns)))
     up = {"tm": lax.rem(t + 1, nt)}
     upper_part = {"space": lax.rem(p + 1, ns)}
@@ -251,8 +239,19 @@
     end_copies = [send_end(0, 0, init_v, pl.ds(0, CUT)), send_end(0, 1, init_v, pl.ds(CUT, E - CUT))]
     know(0)
 
-    for k in range(LAYERS):
-        place[:, layer(k)] = one_hot(column_ids == slots[k])
+    for name in ("nbr", "bnd", "coef", "stiff", "lift", "tlift", "binv"):
+        loads[name].wait()
+
+    def table(ref, f):
+        return jnp.concatenate([ref[f : f + 1, layer(k)] for k in range(8)], axis=0)
+
+    first = p == 0
+    chain_table = jnp.where(first, table(nbr_v, 0), table(nbr_v, 1)) & (E - 1)
+    chain = [jnp.where(first, upper, lower)]
+    for k in range(1, LAYERS):
+        chain.append(lookup(chain_table, chain[-1]))
+    slots = [jnp.where(first, chain[LAYERS - 1 - k], chain[k]) for k in range(LAYERS)]
+
     base_col = column(slots[0])
     top_col = column(slots[LAYERS - 1])
     out_map = one_hot(top_col == upper)
@@ -274,38 +273,36 @@
         for g in range(2)
     ]
 
-    loads["stiff"].wait()
     sh, sl = split(stiff_v[...])
     w_vol[R : R + D, :] = jnp.concatenate([sh, sh, sl], axis=1)
 
-    loads["coef"].wait()
     coef = coef_v[...]
     ch = coef.astype(BF16)
     rest = coef - ch.astype(F32)
     cm = rest.astype(BF16)
     cl = (rest - cm.astype(F32)).astype(BF16)
     xs[2 * D : 2 * D + 16, :] = jnp.concatenate([ch, cm, cl, jnp.zeros((13, E), BF16)], axis=0)
-    moved = dot(xs[...], place[...])
-    coef = moved[2 * D : 2 * D + 1] + moved[2 * D + 1 : 2 * D + 2] + moved[2 * D + 2 : 2 * D + 3]
+    for q in range(4):
+        c = part(q)
+        for k in (2 * q, 2 * q + 1):
+            place[:, layer(k)] = one_hot(column_ids == slots[k])
+        moved = dot(xs[...], place[:, c])
+        coef_v[:, c] = moved[2 * D : 2 * D + 1] + moved[2 * D + 1 : 2 * D + 2] + moved[2 * D + 2 : 2 * D + 3]
+        xh = moved[0:D].astype(BF16)
+        x3[0:D, c] = xh
+        x3[D : 2 * D, c] = moved[D : 2 * D].astype(BF16)
+        x3[2 * D : 3 * D, c] = xh
+        start_v[:, c] = moved[0:H] + moved[D : D + H]
+    coef = coef_v[...]
     inverse_coef = 1.0 / coef
-    xh = moved[0:D].astype(BF16)
-    x3[0:D, :] = xh
-    x3[D : 2 * D, :] = moved[D : 2 * D].astype(BF16)
-    x3[2 * D : 3 * D, :] = xh
-    start = moved[0:H] + moved[D : D + H]
-
-    know(1)
 
     def wide(high, low):
         return jnp.concatenate([high, high, low], axis=0).astype(F32).T.astype(BF16)
 
-    loads["lift"].wait()
     both = dot(to_face, jnp.concatenate(split(lift_v[...]), axis=1))
     w_lift[...] = wide(both[:, :D], both[:, D:])
-    loads["tlift"].wait()
     th, tl = split(tlift_v[...])
     w_time[...] = wide(th, tl)
-    loads["binv"].wait()
     bh, bl = split(binv_v[...])
     w_inv[...] = jnp.concatenate([bh, bh, bl], axis=1)
     both = lax.dot_general(
@@ -344,9 +341,9 @@
         jsplit[...] = stack3(jumps[k, 0:R])
         return coef * work[R : R + D, :] + dot(w_lift[...], jsplit[...])
 
+    know(1)
     work[...] = dot(w_vol[...], x3[...])
     lateral_jumps(0)
-    know(2)
     loads["rhs"].wait()
     moved = dot(jnp.concatenate(split(rhs_v[...]), axis=0), place[...])
     pre[...] = moved[:D] + moved[D:]
@@ -354,32 +351,31 @@
     pre[...] = pre[...] - apply_local(0)
     r3[...] = stack3(pre[...])
     bpre[...] = dot(w_inv[...], r3[...]) * inverse_coef
-    know(3)
 
     end_copies[0].wait_recv()
     moved_end[...] = dot(jnp.concatenate(split(end_in[0, :, 0:CUT]), axis=0), place[0:CUT, :])
     end_copies[1].wait_recv()
     late = jnp.concatenate(split(end_in[0, :, CUT:E]), axis=0)
+    moved = moved_end[...] + dot(late, place[CUT:E, :])
+    jump = start_v[...] - jnp.where(t == 0, 0.0, moved[:H] + moved[H:])
+    jumps[0, R:, :] = jump
+    t3[...] = stack3(jump)
     dir_copies = {}
     for q in PARTS:
         c = part(q)
-        moved = moved_end[:, c] + dot(late, place[CUT:E, c])
-        jump = start[:, c] - jnp.where(t == 0, 0.0, moved[:H] + moved[H:])
-        jumps[0, R:, c] = jump
-        t3[:, c] = stack3(jump)
         direction = bpre[:, c] - dot(w_both[...], t3[:, c]) * inverse_coef[:, c]
         direc[:, c] = direction
         dir_copies[q] = send_end(1, q, direc, pl.ds(q * W, W))
         x3[:, c] = stack3(direction)
-
-    for q in PARTS:
-        work[:, part(q)] = dot(w_vol[...], x3[:, part(q)])
         if q == 3:
-            rim_out[1, 1] = work[0:FD, layer(0)]
-            turned = dot(jnp.concatenate(split(work[FD : 2 * FD, layer(LAYERS - 1)]), axis=0), out_map)
+            rim_out[1, 1] = dot(w_vol[0:FD, :], x3[:, layer(0)])
+            rim = dot(w_vol[FD : 2 * FD, :], x3[:, layer(LAYERS - 1)])
+            turned = dot(jnp.concatenate(split(rim), axis=0), out_map)
             rim_out[1, 0] = turned[:FD] + turned[FD:]
             rims2 = send_rims(1)
-    know(4)
+    know(2)
+
+    work[...] = dot(w_vol[...], x3[...])
     residual = pre[...] - dot(w_time[...], t3[...])
     resid[...] = residual
     rows[2:3, :] = over(residual * residual) + 0.5 * over(jumps[0, :R] * jumps[0, :R]) + over(jumps[0, R:] * jumps[0, R:])
@@ -426,8 +422,10 @@
         others = buf.at[pl.ds(0, count - 1)]
         return pltpu.make_async_copy(others, others, sum_recv.at[n])
 
+    know(3, (0,))
     row_a[t] = message
     got = exchange(row_a, t, nt, "tm", 0)
+    know(3, (1,))
     eh = rows[...].astype(BF16)
     rest = rows[...] - eh.astype(F32)
     em = rest.astype(BF16)
@@ -444,6 +442,7 @@
     total = row_a[0]
     for d in range(1, nt):
         total = total + row_a[d]
+    know(4, (1,))
     row_b[p] = total
     exchange(row_b, p, ns, "space", 1).wait()
     total = row_b[0]
@@ -495,6 +494,7 @@
             vmem((6, E), jnp.int32),
             vmem((2, NB), jnp.int32),
             vmem((E, E), BF16),
+            vmem((H, E), F32),
             vmem((2 * D + 16, E), BF16),
             vmem((3 * D, E), BF16),
             vmem((3 * D, E), BF16),

time: 43.2 us -> 36.9 us (0.85)
  Pallas kernels: 42.4 us -> 36.1 us
    pallas_call x1, Pallas kernels: 41.3 us -> 35 us  [on_device(): pl.pallas_call(functools.partial(kernel, nt, ns), out_shape=(jax.ShapeDty...]
where the time goes in v3:
time: 36.9 us; the launch traced here: 36.8 us
  Pallas kernels  36.1 us (98%)
  between operations  0.66 us (2%)
    pallas_call x1, Pallas kernels, on_device(): pl.pallas_call(functools.partial(kernel, nt, ns), out_shape=(jax.ShapeDty...  35 us
    pallas_call x1, Pallas kernels, on_device(): pl.pallas_call(functools.partial(finish, float(E * nt * ns)), out_shape=(...  1.1 us

profile of v3, /device:TPU:1, one launch (start us, length us, event | category | flops | bytes accessed | tf_op | source)
XLA Modules:
  0.0 36.8 jit_solution(14556215434724918693)
XLA Ops:
  0.6 0.0 copy-start
  0.6 35.0 %shard_map.130 = (f32[128,1024]{1,0:T(8,128)S(1)}, f32[8,1024]{1,0:T(8,128)S(1)}, f32[1,128]{1,0:T(1,128)S(1)}) custom-call(f32[1,128,1024]{2,1,0:T(8,128)} %init_v.1, f32[1,128,1024]{2,1,0:T(8,128)} %rhs_h.1, f32[1,1024]{1,0:T(1,128)} %bitcast.8, f32[128,128]{1,0:T(8,128)} %stiff_h.1, f32[128,128]{1,0:T(8,128)} %binv_h.1, f32[192,128]{1,0:T(8,128)} %fproj_h.1, ...), custom_call_target="tpu_custom_call" | custom-call | flops 4000000000 | bytes 3145728 | tf_op jit(solution)/shard_map/pallas_call | solution.py:475
  35.6 0.0 copy-done
  35.7 1.1 %shard_map.131 = (f32[1,128,1024]{2,1,0:T(8,128)}, f32[1,1024]{1,0:T(1,128)}, f32[1,128]{1,0:T(1,128)}) custom-call(f32[1,128,1024]{2,1,0:T(8,128)S(1)} %copy-done, f32[128,1024]{1,0:T(8,128)S(1)} %get-tuple-element.9.dir_v, f32[8,1024]{1,0:T(8,128)S(1)} %get-tuple-element.10.eta_v, f32[1,128]{1,0:T(1,128)S(1)} %get-tuple-element.11.tot_v), custom_call_target="tpu_custom_call" | custom-call | flops 300000 | bytes 1048576 | tf_op jit(solution)/shard_map/pallas_call | solution.py:551
Async XLA Ops:
  0.6 35.0 %copy-start = (f32[1,128,1024]{2,1,0:T(8,128)S(1)}, f32[1,128,1024]{2,1,0:T(8,128)}, u32[]{:S(2)}) copy-start(f32[1,128,1024]{2,1,0:T(8,128)} %init_v.1) | copy-start | bytes 1572868

commit v4 on v3

--- a/solution.py
+++ b/solution.py
@@ -53,7 +53,7 @@
 
 
 def rounds(n):
-    out, known = [], 1
+    out, known = [], 2
     while known < n // 2:
         out.append(known)
         known *= 2
@@ -61,7 +61,7 @@
 
 
 def near(n):
-    return (1,) if n == 2 else (1, n - 1)
+    return sorted({1, 2, n - 2, n - 1} & set(range(1, n)))
 
 
 def stack3(x):
@@ -73,9 +73,11 @@
     return jnp.sum(x, axis=0, keepdims=True)
 
 
-PARTS = (0, 3, 1, 2)
 W = 256
-CUT = 768
+SIDES = (slice(0, W), slice(E - W, E))
+MIDDLE = slice(W, E - W)
+SIDE_LAYERS = (0, 1, 6, 7)
+MIDDLE_LAYERS = (2, 3, 4, 5)
 
 
 def part(q):
@@ -102,27 +104,20 @@
     init_v,
     rhs_v,
     coef_v,
-    stiff_v,
-    binv_v,
-    fproj_v,
-    lift_v,
-    tlift_v,
-    nbr_v,
-    bnd_v,
+    weights_v,
+    tables_v,
     send_v,
     place,
     start_v,
     xs,
     x3,
-    r3,
     t3,
     work,
     lat,
     jumps,
-    jsplit,
     pre,
     bpre,
-    moved_end,
+    ends_v,
     resid,
     direc,
     rows,
@@ -131,6 +126,7 @@
     w_time,
     w_inv,
     w_both,
+    w_rim,
     rim_out,
     rim_in,
     end_in,
@@ -163,38 +159,91 @@
                 for d in (reach[k], n - reach[k]):
                     pl.semaphore_signal(known_sem.at[base + k], inc=1, device_id={axis: lax.rem(me + d, n)}, device_id_type=MESH)
 
-    loads = {}
-    for n, (name, src, dst) in enumerate(
-        (
-            ("send", send_h, send_v),
-            ("init", init_h.at[0], init_v),
-            ("fproj", fproj_h, fproj_v),
-            ("nbr", nbr_h, nbr_v),
-            ("bnd", bnd_h, bnd_v),
-            ("coef", coef_h, coef_v),
-            ("stiff", stiff_h, stiff_v),
-            ("lift", lift_h, lift_v),
-            ("tlift", tlift_h, tlift_v),
-            ("binv", binv_h, binv_v),
-            ("rhs", rhs_h.at[0], rhs_v),
-        )
+    stiff_v = weights_v.at[pl.ds(0, D)]
+    binv_v = weights_v.at[pl.ds(D, D)]
+    fproj_v = weights_v.at[pl.ds(2 * D, R)]
+    lift_v = weights_v.at[pl.ds(2 * D + R, R)]
+    tlift_v = weights_v.at[pl.ds(2 * D + 2 * R, H)]
+    nbr_v, bnd_v = tables_v.at[0], tables_v.at[1]
+    for n, src, dst in (
+        (0, send_h, send_v),
+        (1, init_h.at[0], init_v),
+        (2, fproj_h, fproj_v),
+        (2, stiff_h, stiff_v),
+        (2, lift_h, lift_v),
+        (2, tlift_h, tlift_v),
+        (2, binv_h, binv_v),
+        (3, nbr_h, nbr_v),
+        (3, bnd_h, bnd_v),
+        (4, coef_h, coef_v),
+        (5, rhs_h.at[0], rhs_v),
     ):
-        loads[name] = pltpu.make_async_copy(src, dst, load_sem.at[n])
-        loads[name].start()
+        pltpu.make_async_copy(src, dst, load_sem.at[n]).start()
+
+    def arrived(ref, sem):
+        pltpu.make_async_copy(ref, ref, sem).wait()
+
+    arrived(send_v, load_sem.at[0])
+    arrived(init_v, load_sem.at[1])
+    arrived(weights_v, load_sem.at[2])
+    arrived(tables_v, load_sem.at[3])
+    arrived(coef_v, load_sem.at[4])
+    up = {"tm": lax.rem(t + 1, nt)}
+    upper_part = {"space": lax.rem(p + 1, ns)}
+    lower_part = {"space": lax.rem(p + ns - 1, ns)}
+
+    def send_end(k, n, src, columns):
+        @pl.when(t < nt - 1)
+        def _():
+            pltpu.make_async_remote_copy(
+                src_ref=src.at[pl.ds(H, H), columns],
+                dst_ref=end_in.at[k, :, columns],
+                send_sem=end_send.at[0],
+                recv_sem=end_recv.at[n],
+                device_id=up,
+                device_id_type=MESH,
+            ).start()
+
+    def end_arrived(ref, n):
+        @pl.when(t > 0)
+        def _():
+            arrived(ref, end_recv.at[n])
+
+    def send_rims(k):
+        for side, device, there in ((0, upper_part, p < ns - 1), (1, lower_part, p > 0)):
+
+            @pl.when(there)
+            def _():
+                pltpu.make_async_remote_copy(
+                    src_ref=rim_out.at[k, side],
+                    dst_ref=rim_in.at[k, side],
+                    send_sem=rim_send.at[side],
+                    recv_sem=rim_recv.at[k, side],
+                    device_id=device,
+                    device_id_type=MESH,
+                ).start()
 
     row, col = iota((R, R), 0), iota((R, R), 1)
     to_face = one_hot(col == (row & 31) * 6 + (row >> 5))
-    loads["send"].wait()
     lower = send_v[0:1, :] & (E - 1)
     upper = send_v[1:2, :] & (E - 1)
     column_ids = iota((E, NB), 0)
     ends = jnp.concatenate([one_hot(column_ids == lower), one_hot(column_ids == upper)], axis=1)
-    loads["fproj"].wait()
     both = dot(to_face, jnp.concatenate(split(fproj_v[...]), axis=1)).astype(BF16)
     fh, fl = both[:, :D], both[:, D:]
     w_vol[0:R, :] = jnp.concatenate([fh, fh, fl], axis=1)
 
-    loads["init"].wait()
+
+    def table(ref, f):
+        return jnp.concatenate([ref[f : f + 1, layer(k)] for k in range(8)], axis=0)
+
+    first = p == 0
+    chain_table = jnp.where(first, table(nbr_v, 0), table(nbr_v, 1)) & (E - 1)
+    chain = [jnp.where(first, upper, lower)]
+    for k in range(1, LAYERS):
+        chain.append(lookup(chain_table, chain[-1]))
+    slots = [jnp.where(first, chain[LAYERS - 1 - k], chain[k]) for k in range(LAYERS)]
+
     ih, il = split(init_v[...])
     xs[0:D, :] = ih
     xs[D : 2 * D, :] = il
@@ -204,53 +253,9 @@
     rim_out[0, 0] = rim[FD : 2 * FD, NB : 2 * NB]
 
     pl.semaphore_wait(barrier, len(near(nt)) + len(near(ns)))
-    up = {"tm": lax.rem(t + 1, nt)}
-    upper_part = {"space": lax.rem(p + 1, ns)}
-    lower_part = {"space": lax.rem(p + ns - 1, ns)}
-
-    def send_end(k, n, src, columns):
-        copy = pltpu.make_async_remote_copy(
-            src_ref=src.at[pl.ds(H, H), columns],
-            dst_ref=end_in.at[k, :, columns],
-            send_sem=end_send.at[k, n],
-            recv_sem=end_recv.at[k, n],
-            device_id=up,
-            device_id_type=MESH,
-        )
-        copy.start()
-        return copy
-
-    def send_rims(k):
-        copies = []
-        for side, device in ((0, upper_part), (1, lower_part)):
-            copy = pltpu.make_async_remote_copy(
-                src_ref=rim_out.at[k, side],
-                dst_ref=rim_in.at[k, side],
-                send_sem=rim_send.at[k, side],
-                recv_sem=rim_recv.at[k, side],
-                device_id=device,
-                device_id_type=MESH,
-            )
-            copy.start()
-            copies.append(copy)
-        return copies
-
-    rims = send_rims(0)
-    end_copies = [send_end(0, 0, init_v, pl.ds(0, CUT)), send_end(0, 1, init_v, pl.ds(CUT, E - CUT))]
+    send_end(0, 0, init_v, pl.ds(0, E))
+    send_rims(0)
     know(0)
-
-    for name in ("nbr", "bnd", "coef", "stiff", "lift", "tlift", "binv"):
-        loads[name].wait()
-
-    def table(ref, f):
-        return jnp.concatenate([ref[f : f + 1, layer(k)] for k in range(8)], axis=0)
-
-    first = p == 0
-    chain_table = jnp.where(first, table(nbr_v, 0), table(nbr_v, 1)) & (E - 1)
-    chain = [jnp.where(first, upper, lower)]
-    for k in range(1, LAYERS):
-        chain.append(lookup(chain_table, chain[-1]))
-    slots = [jnp.where(first, chain[LAYERS - 1 - k], chain[k]) for k in range(LAYERS)]
 
     base_col = column(slots[0])
     top_col = column(slots[LAYERS - 1])
@@ -301,6 +306,7 @@
 
     both = dot(to_face, jnp.concatenate(split(lift_v[...]), axis=1))
     w_lift[...] = wide(both[:, :D], both[:, D:])
+    lift_high, lift_low = both[:, :D].astype(BF16), both[:, D:].astype(BF16)
     th, tl = split(tlift_v[...])
     w_time[...] = wide(th, tl)
     bh, bl = split(binv_v[...])
@@ -309,102 +315,160 @@
         jnp.concatenate([th, tl, th], axis=1), w_inv[...], (((1,), (1,)), ((), ())), preferred_element_type=F32
     )
     w_both[...] = wide(*split(both))
-
-    def lateral_jumps(k):
+    for f in range(2):
+        high, low = lift_high[f * FD : (f + 1) * FD], lift_low[f * FD : (f + 1) * FD]
+        both = lax.dot_general(
+            jnp.concatenate([high, low, high], axis=1), w_inv[...], (((1,), (1,)), ((), ())), preferred_element_type=F32
+        )
+        w_rim[f, 0:D, :] = wide(high, low)
+        w_rim[f, D : 2 * D, :] = wide(*split(both))
+
+    def lateral_jumps(k, layers):
+        count = len(layers) * 2 * FD
         for g in range(2):
             a, b = 2 + 2 * g, 3 + 2 * g
-            for x in range(LAYERS):
+            for n, x in enumerate(layers):
                 for side, f in ((0, b), (1, a)):
                     high, low = split(work[f * FD : (f + 1) * FD, layer(x)])
-                    lat[x * 2 * FD : x * 2 * FD + FD, layer(side)] = high
-                    lat[x * 2 * FD + FD : (x + 1) * 2 * FD, layer(side)] = low
-            seen = dot(lat[...], lat_maps[g])
-            for x in range(LAYERS):
-                both = seen[x * 2 * FD : x * 2 * FD + FD] + seen[x * 2 * FD + FD : (x + 1) * 2 * FD]
+                    lat[n * 2 * FD : n * 2 * FD + FD, layer(side)] = high
+                    lat[n * 2 * FD + FD : (n + 1) * 2 * FD, layer(side)] = low
+            seen = dot(lat[0:count], lat_maps[g])
+            for n, x in enumerate(layers):
+                both = seen[n * 2 * FD : n * 2 * FD + FD] + seen[n * 2 * FD + FD : (n + 1) * 2 * FD]
                 for side, f in ((0, a), (1, b)):
                     jumps[k, f * FD : (f + 1) * FD, layer(x)] = work[f * FD : (f + 1) * FD, layer(x)] - both[:, layer(side)]
-        for x in range(1, LAYERS):
-            jumps[k, 0:FD, layer(x)] = work[0:FD, layer(x)] - work[FD : 2 * FD, layer(x - 1)]
-            jumps[k, FD : 2 * FD, layer(x - 1)] = work[FD : 2 * FD, layer(x - 1)] - work[0:FD, layer(x)]
-
-    def rim_jumps(k, copies):
-        copies[0].wait_recv()
-        copies[1].wait_recv()
-        from_lower = jnp.where(p == 0, 0.0, rim_in[k, 0])
-        jumps[k, 0:FD, layer(0)] = work[0:FD, layer(0)] - from_lower
+        for x in layers:
+            if x > 0:
+                jumps[k, 0:FD, layer(x)] = work[0:FD, layer(x)] - work[FD : 2 * FD, layer(x - 1)]
+            if x < LAYERS - 1:
+                jumps[k, FD : 2 * FD, layer(x)] = work[FD : 2 * FD, layer(x)] - work[0:FD, layer(x + 1)]
+
+    rim_blocks = ((0, layer(0)), (1, layer(LAYERS - 1)))
+
+    def without_rims(k):
+        for f, c in rim_blocks:
+            jumps[k, f * FD : (f + 1) * FD, c] = jnp.zeros((FD, NB), F32)
+
+    def rims_arrived(k):
+        for side, there in ((0, p > 0), (1, p < ns - 1)):
+
+            @pl.when(there)
+            def _():
+                arrived(rim_in.at[k, side], rim_recv.at[k, side])
+
+    def rim_terms(k):
         turned = dot(jnp.concatenate(split(rim_in[k, 1]), axis=0), in_map)
-        from_upper = jnp.where(p == ns - 1, 0.0, turned[:FD] + turned[FD:])
-        last = layer(LAYERS - 1)
-        jumps[k, FD : 2 * FD, last] = work[FD : 2 * FD, last] - from_upper
-
-    def apply_local(k):
-        jsplit[...] = stack3(jumps[k, 0:R])
-        return coef * work[R : R + D, :] + dot(w_lift[...], jsplit[...])
-
+        outside = (
+            jnp.where(p == 0, 0.0, rim_in[k, 0]),
+            jnp.where(p == ns - 1, 0.0, turned[:FD] + turned[FD:]),
+        )
+        found = []
+        for f, c in rim_blocks:
+            block = work[f * FD : (f + 1) * FD, c] - outside[f]
+            jumps[k, f * FD : (f + 1) * FD, c] = block
+            added = dot(w_rim[f, 0 : D if k else 2 * D, :], stack3(block))
+            found.append((f, c, block, added))
+        return found
+
+    def apply_local(k, c):
+        return coef[:, c] * work[R : R + D, c] + dot(w_lift[...], stack3(jumps[k, 0:R, c]))
+
+    def move_rhs(c):
+        moved = dot(xs[0 : 2 * D, :], place[:, c])
+        pre[:, c] = moved[:D] + moved[D:]
+
+    def start_residual(c):
+        local = pre[:, c] - apply_local(0, c)
+        pre[:, c] = local
+        bpre[:, c] = dot(w_inv[...], stack3(local)) * inverse_coef[:, c]
+
+    arrived(rhs_v, load_sem.at[5])
+    work[...] = dot(w_vol[...], x3[...])
+    rh, rl = split(rhs_v[...])
+    xs[0:D, :] = rh
+    xs[D : 2 * D, :] = rl
+    lateral_jumps(0, SIDE_LAYERS)
+    for c in SIDES:
+        move_rhs(c)
+    without_rims(0)
+    for c in SIDES:
+        start_residual(c)
+
+    end_arrived(end_in.at[0], 0)
+    eh, el = split(end_in[0])
+    ends_v[0:H, :] = eh
+    ends_v[H : 2 * H, :] = el
+
+    def slab_start(c):
+        moved = dot(ends_v[...], place[:, c])
+        jump = start_v[:, c] - jnp.where(t == 0, 0.0, moved[:H] + moved[H:])
+        jumps[0, R:, c] = jump
+        t3[:, c] = stack3(jump)
+        direc[:, c] = bpre[:, c] - dot(w_both[...], t3[:, c]) * inverse_coef[:, c]
+
+    for c in SIDES:
+        slab_start(c)
+    rims_arrived(0)
     know(1)
-    work[...] = dot(w_vol[...], x3[...])
-    lateral_jumps(0)
-    loads["rhs"].wait()
-    moved = dot(jnp.concatenate(split(rhs_v[...]), axis=0), place[...])
-    pre[...] = moved[:D] + moved[D:]
-    rim_jumps(0, rims)
-    pre[...] = pre[...] - apply_local(0)
-    r3[...] = stack3(pre[...])
-    bpre[...] = dot(w_inv[...], r3[...]) * inverse_coef
-
-    end_copies[0].wait_recv()
-    moved_end[...] = dot(jnp.concatenate(split(end_in[0, :, 0:CUT]), axis=0), place[0:CUT, :])
-    end_copies[1].wait_recv()
-    late = jnp.concatenate(split(end_in[0, :, CUT:E]), axis=0)
-    moved = moved_end[...] + dot(late, place[CUT:E, :])
-    jump = start_v[...] - jnp.where(t == 0, 0.0, moved[:H] + moved[H:])
-    jumps[0, R:, :] = jump
-    t3[...] = stack3(jump)
-    dir_copies = {}
-    for q in PARTS:
-        c = part(q)
-        direction = bpre[:, c] - dot(w_both[...], t3[:, c]) * inverse_coef[:, c]
-        direc[:, c] = direction
-        dir_copies[q] = send_end(1, q, direc, pl.ds(q * W, W))
-        x3[:, c] = stack3(direction)
-        if q == 3:
-            rim_out[1, 1] = dot(w_vol[0:FD, :], x3[:, layer(0)])
-            rim = dot(w_vol[FD : 2 * FD, :], x3[:, layer(LAYERS - 1)])
-            turned = dot(jnp.concatenate(split(rim), axis=0), out_map)
-            rim_out[1, 0] = turned[:FD] + turned[FD:]
-            rims2 = send_rims(1)
-    know(2)
+    for _, c, _, added in rim_terms(0):
+        pre[:, c] = pre[:, c] - added[:D]
+        direc[:, c] = direc[:, c] - added[D:] * inverse_coef[:, c]
+    for c in SIDES:
+        x3[:, c] = stack3(direc[:, c])
+    for n, c in enumerate(SIDES):
+        send_end(1, 1 + n, direc, pl.ds(c.start, W))
+    rim_out[1, 1] = dot(w_vol[0:FD, :], x3[:, layer(0)])
+    rim = dot(w_vol[FD : 2 * FD, :], x3[:, layer(LAYERS - 1)])
+    turned = dot(jnp.concatenate(split(rim), axis=0), out_map)
+    rim_out[1, 0] = turned[:FD] + turned[FD:]
+    send_rims(1)
+    lateral_jumps(0, MIDDLE_LAYERS)
+    move_rhs(MIDDLE)
+    start_residual(MIDDLE)
+    slab_start(MIDDLE)
+    x3[:, MIDDLE] = stack3(direc[:, MIDDLE])
+    send_end(1, 3, direc, pl.ds(W, E - 2 * W))
 
     work[...] = dot(w_vol[...], x3[...])
     residual = pre[...] - dot(w_time[...], t3[...])
     resid[...] = residual
-    rows[2:3, :] = over(residual * residual) + 0.5 * over(jumps[0, :R] * jumps[0, :R]) + over(jumps[0, R:] * jumps[0, R:])
-    lateral_jumps(1)
-    rim_jumps(1, rims2)
-    pre[...] = apply_local(1)
-    mixed = over(jumps[0, :R] * jumps[1, :R])
-    quad = 0.5 * over(jumps[1, :R] * jumps[1, :R])
-    folded = jnp.zeros((8, NB), F32)
-    for q in PARTS:
-        c = part(q)
-        dir_copies[q].wait_recv()
+    lateral_jumps(1, SIDE_LAYERS + MIDDLE_LAYERS)
+    without_rims(1)
+    pre[...] = apply_local(1, slice(0, E))
+    j0, j1 = jumps[0, :R], jumps[1, :R]
+    rows[2:3, :] = over(residual * residual) + 0.5 * over(j0 * j0) + over(jumps[0, R:] * jumps[0, R:])
+    rows[3:4, :] = over(j0 * j1)
+    rows[4:5, :] = 0.5 * over(j1 * j1)
+    rims_arrived(1)
+    for f, c, block, added in rim_terms(1):
+        pre[:, c] = pre[:, c] + added
+        rows[3:4, c] = rows[3:4, c] + over(jumps[0, f * FD : (f + 1) * FD, c] * block)
+        rows[4:5, c] = rows[4:5, c] + 0.5 * over(block * block)
+
+    def image_sums(c):
         jump = direc[0:H, c] - jnp.where(t == 0, 0.0, end_in[1, :, c])
         image = pre[:, c] + dot(w_time[...], stack3(jump))
         cross = over(resid[:, c] * image)
         square = over(image * image)
-        part_rows = jnp.concatenate(
+        found = jnp.concatenate(
             [
                 cross,
                 square,
                 rows[2:3, c],
-                mixed[:, c] + 2.0 * over(jumps[0, R:, c] * jump) - 2.0 * cross,
-                quad[:, c] + square + over(jump * jump),
-                jnp.zeros((3, W), F32),
+                rows[3:4, c] + 2.0 * over(jumps[0, R:, c] * jump) - 2.0 * cross,
+                rows[4:5, c] + square + over(jump * jump),
+                jnp.zeros((3, c.stop - c.start), F32),
             ],
             axis=0,
         )
-        rows[:, c] = part_rows
-        folded = folded + part_rows[:, :NB] + part_rows[:, NB:]
+        rows[:, c] = found
+        return sum(found[:, layer(k)] for k in range((c.stop - c.start) // NB))
+
+    for n, c in enumerate(SIDES):
+        end_arrived(end_in.at[1, :, pl.ds(c.start, W)], 1 + n)
+    folded = image_sums(SIDES[0]) + image_sums(SIDES[1])
+    end_arrived(end_in.at[1, :, pl.ds(W, E - 2 * W)], 3)
+    folded = folded + image_sums(MIDDLE)
     sums = jnp.sum(folded, axis=1, keepdims=True)
     diagonal = iota((8, NB), 0) == iota((8, NB), 1)
     message = jnp.sum(jnp.where(diagonal, sums, 0.0), axis=0, keepdims=True)
@@ -414,7 +478,7 @@
             pltpu.make_async_remote_copy(
                 src_ref=buf.at[me],
                 dst_ref=buf.at[me],
-                send_sem=sum_send.at[n],
+                send_sem=sum_send.at[0],
                 recv_sem=sum_recv.at[n],
                 device_id={axis: lax.rem(me + d, count)},
                 device_id_type=MESH,
@@ -422,10 +486,10 @@
         others = buf.at[pl.ds(0, count - 1)]
         return pltpu.make_async_copy(others, others, sum_recv.at[n])
 
-    know(3, (0,))
+    know(2, (0,))
     row_a[t] = message
     got = exchange(row_a, t, nt, "tm", 0)
-    know(3, (1,))
+    know(2, (1,))
     eh = rows[...].astype(BF16)
     rest = rows[...] - eh.astype(F32)
     em = rest.astype(BF16)
@@ -442,7 +506,7 @@
     total = row_a[0]
     for d in range(1, nt):
         total = total + row_a[d]
-    know(4, (1,))
+    know(3, (1,))
     row_b[p] = total
     exchange(row_b, p, ns, "space", 1).wait()
     total = row_b[0]
@@ -450,11 +514,17 @@
         total = total + row_b[d]
     tot_o[...] = total
 
-    for copy in end_copies + [dir_copies[q] for q in PARTS] + rims + rims2:
-        copy.wait_send()
-    for buf, count, n in ((row_a, nt, 0), (row_b, ns, 1)):
-        sent = buf.at[pl.ds(0, count - 1)]
-        pltpu.make_async_copy(sent, sent, sum_send.at[n]).wait()
+    @pl.when(t < nt - 1)
+    def _():
+        arrived(end_in, end_send.at[0])
+
+    for side, there in ((0, p < ns - 1), (1, p > 0)):
+
+        @pl.when(there)
+        def _():
+            arrived(rim_in.at[:, side], rim_send.at[side])
+
+    arrived(row_b.at[pl.ds(0, nt + ns - 2)], sum_send.at[0])
 
 
 def finish(count, init_v, dir_v, eta_v, tot_v, out_o, ind_o, est_o):
@@ -485,27 +555,20 @@
             vmem((D, E), F32),
             vmem((D, E), F32),
             vmem((1, E), F32),
-            vmem((D, D), F32),
-            vmem((D, D), F32),
-            vmem((R, D), F32),
-            vmem((R, D), F32),
-            vmem((H, D), F32),
-            vmem((6, E), jnp.int32),
-            vmem((6, E), jnp.int32),
+            vmem((2 * D + 2 * R + H, D), F32),
+            vmem((2, 6, E), jnp.int32),
             vmem((2, NB), jnp.int32),
             vmem((E, E), BF16),
             vmem((H, E), F32),
             vmem((2 * D + 16, E), BF16),
             vmem((3 * D, E), BF16),
-            vmem((3 * D, E), BF16),
             vmem((3 * H, E), BF16),
             vmem((R + D, E), F32),
             vmem((LAYERS * 2 * FD, 2 * NB), BF16),
             vmem((2, 256, E), F32),
-            vmem((3 * R, E), BF16),
             vmem((D, E), F32),
             vmem((D, E), F32),
-            vmem((2 * H, E), F32),
+            vmem((2 * H, E), BF16),
             vmem((D, E), F32),
             vmem((D, E), F32),
             vmem((8, E), F32),
@@ -514,17 +577,18 @@
             vmem((D, 3 * H), BF16),
             vmem((D, 3 * D), BF16),
             vmem((D, 3 * H), BF16),
+            vmem((2, 2 * D, 3 * FD), BF16),
             vmem((2, 2, FD, NB), F32),
             vmem((2, 2, FD, NB), F32),
             vmem((2, H, E), F32),
             vmem((nt, 1, NB), F32),
-            vmem((ns, 1, NB), F32),
-            dma((11,)),
-            dma((2, 4)),
-            dma((2, 4)),
+            vmem((nt + ns, 1, NB), F32),
+            dma((6,)),
+            dma((1,)),
+            dma((4,)),
+            dma((2,)),
             dma((2, 2)),
-            dma((2, 2)),
-            dma((2,)),
+            dma((1,)),
             dma((2,)),
             pltpu.SemaphoreType.REGULAR((max(1, len(rounds(nt)) + len(rounds(ns))),)),
         ],

time: 36.9 us -> 35.9 us (0.973)
  Pallas kernels: 36.1 us -> 35.1 us
    pallas_call x1, Pallas kernels: 35 us -> 34 us  [on_device(): pl.pallas_call(functools.partial(kernel, nt, ns), out_shape=(jax.ShapeDty...]
where the time goes in v4:
time: 35.9 us; the launch traced here: 35.8 us
  Pallas kernels  35.1 us (98%)
  between operations  0.66 us (2%)
    pallas_call x1, Pallas kernels, on_device(): pl.pallas_call(functools.partial(kernel, nt, ns), out_shape=(jax.ShapeDty...  34 us
    pallas_call x1, Pallas kernels, on_device(): pl.pallas_call(functools.partial(finish, float(E * nt * ns)), out_shape=(...  1.1 us

profile of v4, /device:TPU:1, one launch (start us, length us, event | category | flops | bytes accessed | tf_op | source)
XLA Modules:
  0.0 35.8 jit_solution(6378780783912832617)
XLA Ops:
  0.6 0.0 copy-start
  0.6 34.0 %shard_map.130 = (f32[128,1024]{1,0:T(8,128)S(1)}, f32[8,1024]{1,0:T(8,128)S(1)}, f32[1,128]{1,0:T(1,128)S(1)}) custom-call(f32[1,128,1024]{2,1,0:T(8,128)} %init_v.1, f32[1,128,1024]{2,1,0:T(8,128)} %rhs_h.1, f32[1,1024]{1,0:T(1,128)} %bitcast.8, f32[128,128]{1,0:T(8,128)} %stiff_h.1, f32[128,128]{1,0:T(8,128)} %binv_h.1, f32[192,128]{1,0:T(8,128)} %fproj_h.1, ...), custom_call_target="tpu_custom_call" | custom-call | flops 4000000000 | bytes 3145728 | tf_op jit(solution)/shard_map/pallas_call | solution.py:545
  34.7 0.0 copy-done
  34.7 1.1 %shard_map.131 = (f32[1,128,1024]{2,1,0:T(8,128)}, f32[1,1024]{1,0:T(1,128)}, f32[1,128]{1,0:T(1,128)}) custom-call(f32[1,128,1024]{2,1,0:T(8,128)S(1)} %copy-done, f32[128,1024]{1,0:T(8,128)S(1)} %get-tuple-element.9.dir_v, f32[8,1024]{1,0:T(8,128)S(1)} %get-tuple-element.10.eta_v, f32[1,128]{1,0:T(1,128)S(1)} %get-tuple-element.11.tot_v), custom_call_target="tpu_custom_call" | custom-call | flops 300000 | bytes 1048576 | tf_op jit(solution)/shard_map/pallas_call | solution.py:615
Async XLA Ops:
  0.6 34.0 %copy-start = (f32[1,128,1024]{2,1,0:T(8,128)S(1)}, f32[1,128,1024]{2,1,0:T(8,128)}, u32[]{:S(2)}) copy-start(f32[1,128,1024]{2,1,0:T(8,128)} %init_v.1) | copy-start | bytes 1572868

commit v5 on v4

--- a/solution.py
+++ b/solution.py
@@ -52,16 +52,21 @@
     return slice(k * NB, (k + 1) * NB)
 
 
-def rounds(n):
-    out, known = [], 2
+def rounds(n, known):
+    out = []
     while known < n // 2:
         out.append(known)
         known *= 2
     return out
 
 
-def near(n):
-    return sorted({1, 2, n - 2, n - 1} & set(range(1, n)))
+def near(n, radius):
+    return [d for d in range(1, n) if min(d, n - d) <= radius]
+
+
+TM_RADIUS, SPACE_RADIUS = 2, 1
+CUT = 768
+OUT_PARTS = 2
 
 
 def stack3(x):
@@ -98,10 +103,10 @@
     nbr_h,
     bnd_h,
     send_h,
+    init_v,
     dir_o,
     eta_o,
     tot_o,
-    init_v,
     rhs_v,
     coef_v,
     weights_v,
@@ -118,6 +123,8 @@
     pre,
     bpre,
     ends_v,
+    moved_v,
+    folded_v,
     resid,
     direc,
     rows,
@@ -143,21 +150,21 @@
 ):
     t = lax.axis_index("tm")
     p = lax.axis_index("space")
-    axes = (("tm", t, nt, 0), ("space", p, ns, len(rounds(nt))))
+    tm_rounds, space_rounds = rounds(nt, TM_RADIUS), rounds(ns, SPACE_RADIUS)
+    tm_near, space_near = near(nt, TM_RADIUS), near(ns, SPACE_RADIUS)
 
     barrier = pltpu.get_barrier_semaphore()
-    for axis, me, n, _ in axes:
-        for d in near(n):
+    for axis, me, n, close in (("tm", t, nt, tm_near), ("space", p, ns, space_near)):
+        for d in close:
             pl.semaphore_signal(barrier, inc=1, device_id={axis: lax.rem(me + d, n)}, device_id_type=MESH)
 
-    def know(k, among=(0, 1)):
-        for axis, me, n, base in (axes[i] for i in among):
-            reach = rounds(n)
-            if 0 < k <= len(reach):
-                pl.semaphore_wait(known_sem.at[base + k - 1], 2)
-            if k < len(reach):
-                for d in (reach[k], n - reach[k]):
-                    pl.semaphore_signal(known_sem.at[base + k], inc=1, device_id={axis: lax.rem(me + d, n)}, device_id_type=MESH)
+    def know(axis, k):
+        me, n, reach, base = (t, nt, tm_rounds, 0) if axis == "tm" else (p, ns, space_rounds, len(tm_rounds))
+        if 0 < k <= len(reach):
+            pl.semaphore_wait(known_sem.at[base + k - 1], 2)
+        if k < len(reach):
+            for d in (reach[k], n - reach[k]):
+                pl.semaphore_signal(known_sem.at[base + k], inc=1, device_id={axis: lax.rem(me + d, n)}, device_id_type=MESH)
 
     stiff_v = weights_v.at[pl.ds(0, D)]
     binv_v = weights_v.at[pl.ds(D, D)]
@@ -223,6 +230,10 @@
                     device_id_type=MESH,
                 ).start()
 
+    pl.semaphore_wait(barrier, len(tm_near) + len(space_near))
+    send_end(0, 0, init_v, pl.ds(0, CUT))
+    send_end(0, 4, init_v, pl.ds(CUT, E - CUT))
+
     row, col = iota((R, R), 0), iota((R, R), 1)
     to_face = one_hot(col == (row & 31) * 6 + (row >> 5))
     lower = send_v[0:1, :] & (E - 1)
@@ -252,10 +263,9 @@
     rim_out[0, 1] = rim[0:FD, 0:NB]
     rim_out[0, 0] = rim[FD : 2 * FD, NB : 2 * NB]
 
-    pl.semaphore_wait(barrier, len(near(nt)) + len(near(ns)))
-    send_end(0, 0, init_v, pl.ds(0, E))
     send_rims(0)
-    know(0)
+    know("tm", 0)
+    know("space", 0)
 
     base_col = column(slots[0])
     top_col = column(slots[LAYERS - 1])
@@ -394,13 +404,24 @@
     for c in SIDES:
         start_residual(c)
 
-    end_arrived(end_in.at[0], 0)
-    eh, el = split(end_in[0])
-    ends_v[0:H, :] = eh
-    ends_v[H : 2 * H, :] = el
+    know("tm", 1)
+    know("space", 1)
+    def take_ends(first, last):
+        eh, el = split(end_in[0, :, first:last])
+        ends_v[0:H, first:last] = eh
+        ends_v[H : 2 * H, first:last] = el
+
+    end_arrived(end_in.at[0, :, pl.ds(0, CUT)], 0)
+    take_ends(0, CUT)
+    for c in SIDES:
+        moved_v[:, c] = dot(ends_v[:, 0:CUT], place[0:CUT, c])
+    end_arrived(end_in.at[0, :, pl.ds(CUT, E - CUT)], 4)
+    take_ends(CUT, E)
+    for c in SIDES:
+        moved_v[:, c] = moved_v[:, c] + dot(ends_v[:, CUT:E], place[CUT:E, c])
 
     def slab_start(c):
-        moved = dot(ends_v[...], place[:, c])
+        moved = moved_v[:, c]
         jump = start_v[:, c] - jnp.where(t == 0, 0.0, moved[:H] + moved[H:])
         jumps[0, R:, c] = jump
         t3[:, c] = stack3(jump)
@@ -409,7 +430,6 @@
     for c in SIDES:
         slab_start(c)
     rims_arrived(0)
-    know(1)
     for _, c, _, added in rim_terms(0):
         pre[:, c] = pre[:, c] - added[:D]
         direc[:, c] = direc[:, c] - added[D:] * inverse_coef[:, c]
@@ -425,9 +445,11 @@
     lateral_jumps(0, MIDDLE_LAYERS)
     move_rhs(MIDDLE)
     start_residual(MIDDLE)
+    moved_v[:, MIDDLE] = dot(ends_v[...], place[:, MIDDLE])
     slab_start(MIDDLE)
     x3[:, MIDDLE] = stack3(direc[:, MIDDLE])
     send_end(1, 3, direc, pl.ds(W, E - 2 * W))
+    know("space", 2)
 
     work[...] = dot(w_vol[...], x3[...])
     residual = pre[...] - dot(w_time[...], t3[...])
@@ -439,12 +461,6 @@
     rows[2:3, :] = over(residual * residual) + 0.5 * over(j0 * j0) + over(jumps[0, R:] * jumps[0, R:])
     rows[3:4, :] = over(j0 * j1)
     rows[4:5, :] = 0.5 * over(j1 * j1)
-    rims_arrived(1)
-    for f, c, block, added in rim_terms(1):
-        pre[:, c] = pre[:, c] + added
-        rows[3:4, c] = rows[3:4, c] + over(jumps[0, f * FD : (f + 1) * FD, c] * block)
-        rows[4:5, c] = rows[4:5, c] + 0.5 * over(block * block)
-
     def image_sums(c):
         jump = direc[0:H, c] - jnp.where(t == 0, 0.0, end_in[1, :, c])
         image = pre[:, c] + dot(w_time[...], stack3(jump))
@@ -464,11 +480,31 @@
         rows[:, c] = found
         return sum(found[:, layer(k)] for k in range((c.stop - c.start) // NB))
 
+    def middle_sums():
+        end_arrived(end_in.at[1, :, pl.ds(W, E - 2 * W)], 3)
+        folded_v[...] = image_sums(MIDDLE)
+
+    rims_last = lax.rem(p, LAYERS) == 0
+
+    @pl.when(rims_last)
+    def _():
+        middle_sums()
+
     for n, c in enumerate(SIDES):
         end_arrived(end_in.at[1, :, pl.ds(c.start, W)], 1 + n)
+    rims_arrived(1)
+    for f, c, block, added in rim_terms(1):
+        pre[:, c] = pre[:, c] + added
+        rows[3:4, c] = rows[3:4, c] + over(jumps[0, f * FD : (f + 1) * FD, c] * block)
+        rows[4:5, c] = rows[4:5, c] + 0.5 * over(block * block)
+
     folded = image_sums(SIDES[0]) + image_sums(SIDES[1])
-    end_arrived(end_in.at[1, :, pl.ds(W, E - 2 * W)], 3)
-    folded = folded + image_sums(MIDDLE)
+
+    @pl.when(jnp.logical_not(rims_last))
+    def _():
+        middle_sums()
+
+    folded = folded + folded_v[...]
     sums = jnp.sum(folded, axis=1, keepdims=True)
     diagonal = iota((8, NB), 0) == iota((8, NB), 1)
     message = jnp.sum(jnp.where(diagonal, sums, 0.0), axis=0, keepdims=True)
@@ -486,10 +522,9 @@
         others = buf.at[pl.ds(0, count - 1)]
         return pltpu.make_async_copy(others, others, sum_recv.at[n])
 
-    know(2, (0,))
+    know("tm", 2)
     row_a[t] = message
     got = exchange(row_a, t, nt, "tm", 0)
-    know(2, (1,))
     eh = rows[...].astype(BF16)
     rest = rows[...] - eh.astype(F32)
     em = rest.astype(BF16)
@@ -502,11 +537,12 @@
     )
     dir_o[...] = back[:D] + back[D : 2 * D]
     eta_o[...] = back[2 * D : 2 * D + 8] + back[2 * D + 8 : 2 * D + 16] + back[2 * D + 16 : 2 * D + 24]
+    know("space", 3)
     got.wait()
     total = row_a[0]
     for d in range(1, nt):
         total = total + row_a[d]
-    know(3, (1,))
+    know("space", 4)
     row_b[p] = total
     exchange(row_b, p, ns, "space", 1).wait()
     total = row_b[0]
@@ -527,14 +563,27 @@
     arrived(row_b.at[pl.ds(0, nt + ns - 2)], sum_send.at[0])
 
 
-def finish(count, init_v, dir_v, eta_v, tot_v, out_o, ind_o, est_o):
+def finish(count, init_v, dir_v, eta_v, tot_v, out_h, ind_h, est_h, out_v, ind_v, est_v, sem):
     cross, square, base, mixed, quad = (tot_v[0:1, k : k + 1] for k in range(5))
     step = cross / square
+    copies = []
+
+    def send(src, dst):
+        copies.append(pltpu.make_async_copy(src, dst, sem.at[len(copies)]))
+        copies[-1].start()
+
+    for k in range(OUT_PARTS):
+        part_rows = pl.ds(k * (D // OUT_PARTS), D // OUT_PARTS)
+        out_v[part_rows] = init_v[part_rows] + step * dir_v[part_rows]
+        send(out_v.at[part_rows], out_h.at[0, part_rows])
     eta_total = base + step * mixed + step * step * quad
-    out_o[0] = init_v[0] + step * dir_v[...]
     eta = eta_v[2:3] + step * eta_v[3:4] + step * step * eta_v[4:5]
-    ind_o[...] = eta * count / eta_total
-    est_o[...] = jnp.broadcast_to(jnp.sqrt(eta_total / count), (1, NB))
+    ind_v[...] = eta * count / eta_total
+    send(ind_v, ind_h)
+    est_v[...] = jnp.broadcast_to(jnp.sqrt(eta_total / count), (1, NB))
+    send(est_v, est_h)
+    for copy in copies:
+        copy.wait()
 
 
 def on_device(nt, ns, initial, rhs, coef, stiffness, block_inverse, face_proj, lift, time_lift, neighbour, boundary, send_list):
@@ -542,17 +591,17 @@
     hbm_spec = pl.BlockSpec(memory_space=pltpu.HBM)
     vmem_spec = pl.BlockSpec(memory_space=vmem)
     dma = pltpu.SemaphoreType.DMA
-    direction, eta, totals = pl.pallas_call(
+    iterate, direction, eta, totals = pl.pallas_call(
         functools.partial(kernel, nt, ns),
         out_shape=(
+            jax.ShapeDtypeStruct((D, E), F32),
             jax.ShapeDtypeStruct((D, E), F32),
             jax.ShapeDtypeStruct((8, E), F32),
             jax.ShapeDtypeStruct((1, NB), F32),
         ),
         in_specs=[hbm_spec] * 11,
-        out_specs=[vmem_spec] * 3,
+        out_specs=[vmem_spec] * 4,
         scratch_shapes=[
-            vmem((D, E), F32),
             vmem((D, E), F32),
             vmem((1, E), F32),
             vmem((2 * D + 2 * R + H, D), F32),
@@ -569,6 +618,8 @@
             vmem((D, E), F32),
             vmem((D, E), F32),
             vmem((2 * H, E), BF16),
+            vmem((2 * H, E), F32),
+            vmem((8, NB), F32),
             vmem((D, E), F32),
             vmem((D, E), F32),
             vmem((8, E), F32),
@@ -585,12 +636,12 @@
             vmem((nt + ns, 1, NB), F32),
             dma((6,)),
             dma((1,)),
-            dma((4,)),
+            dma((5,)),
             dma((2,)),
             dma((2, 2)),
             dma((1,)),
             dma((2,)),
-            pltpu.SemaphoreType.REGULAR((max(1, len(rounds(nt)) + len(rounds(ns))),)),
+            pltpu.SemaphoreType.REGULAR((max(1, len(rounds(nt, TM_RADIUS)) + len(rounds(ns, SPACE_RADIUS))),)),
         ],
         compiler_params=pltpu.CompilerParams(collective_id=0, has_side_effects=True, vmem_limit_bytes=40 * 1024 * 1024),
         cost_estimate=pl.CostEstimate(flops=4 * 10**9, bytes_accessed=3 * 2**20, transcendentals=0),
@@ -620,10 +671,16 @@
             jax.ShapeDtypeStruct((1, NB), F32),
         ),
         in_specs=[vmem_spec] * 4,
-        out_specs=[vmem_spec] * 3,
+        out_specs=[hbm_spec] * 3,
+        scratch_shapes=[
+            vmem((D, E), F32),
+            vmem((1, E), F32),
+            vmem((1, NB), F32),
+            dma((OUT_PARTS + 2,)),
+        ],
         compiler_params=pltpu.CompilerParams(vmem_limit_bytes=8 * 1024 * 1024),
         cost_estimate=pl.CostEstimate(flops=3 * 10**5, bytes_accessed=2**20, transcendentals=0),
-    )(initial, direction, eta, totals)
+    )(iterate, direction, eta, totals)
     return smoothed, indicator, estimate[0, :1]
 
 

time: 35.9 us -> 35.4 us (0.986)
  Pallas kernels: 35.1 us -> 34.7 us
    pallas_call x1, Pallas kernels: 34 us -> 33.6 us  [on_device(): pl.pallas_call(functools.partial(kernel, nt, ns), out_shape=(jax.ShapeDty...]
where the time goes in v5:
time: 35.4 us; the launch traced here: 35.3 us
  Pallas kernels  34.7 us (98%)
  between operations  0.64 us (2%)
    pallas_call x1, Pallas kernels, on_device(): pl.pallas_call(functools.partial(kernel, nt, ns), out_shape=(jax.ShapeDty...  33.6 us
    pallas_call x1, Pallas kernels, on_device(): pl.pallas_call(functools.partial(finish, float(E * nt * ns)), out_shape=(...  1.08 us

profile of v5, /device:TPU:1, one launch (start us, length us, event | category | flops | bytes accessed | tf_op | source)
XLA Modules:
  0.0 35.3 jit_solution(11517251452205767919)
XLA Ops:
  0.6 33.6 %shard_map.130 = (f32[128,1024]{1,0:T(8,128)S(1)}, f32[128,1024]{1,0:T(8,128)S(1)}, f32[8,1024]{1,0:T(8,128)S(1)}, f32[1,128]{1,0:T(1,128)S(1)}) custom-call(f32[1,128,1024]{2,1,0:T(8,128)} %init_h.1, f32[1,128,1024]{2,1,0:T(8,128)} %rhs_h.1, f32[1,1024]{1,0:T(1,128)} %bitcast.8, f32[128,128]{1,0:T(8,128)} %stiff_h.1, f32[128,128]{1,0:T(8,128)} %binv_h.1, ...), custom_call_target="tpu_custom_call" | custom-call | flops 4000000000 | bytes 3145728 | tf_op jit(solution)/shard_map/pallas_call | solution.py:594
  34.2 1.1 %shard_map.131 = (f32[1,128,1024]{2,1,0:T(8,128)}, f32[1,1024]{1,0:T(1,128)}, f32[1,128]{1,0:T(1,128)}) custom-call(f32[128,1024]{1,0:T(8,128)S(1)} %get-tuple-element.10.init_v, f32[128,1024]{1,0:T(8,128)S(1)} %get-tuple-element.11.dir_v, f32[8,1024]{1,0:T(8,128)S(1)} %get-tuple-element.12.eta_v, f32[1,128]{1,0:T(1,128)S(1)} %get-tuple-element.13.tot_v), custom_call_target="tpu_custom_call" | custom-call | flops 300000 | bytes 1048576 | tf_op jit(solution)/shard_map/pallas_call | solution.py:666

commit v6 on v5

--- a/solution.py
+++ b/solution.py
@@ -65,7 +65,6 @@
 
 
 TM_RADIUS, SPACE_RADIUS = 2, 1
-CUT = 768
 OUT_PARTS = 2
 
 
@@ -78,15 +77,15 @@
     return jnp.sum(x, axis=0, keepdims=True)
 
 
-W = 256
+W = NB
 SIDES = (slice(0, W), slice(E - W, E))
-MIDDLE = slice(W, E - W)
-SIDE_LAYERS = (0, 1, 6, 7)
-MIDDLE_LAYERS = (2, 3, 4, 5)
+HALVES = (slice(W, 4 * W), slice(4 * W, E - W))
+SIDE_LAYERS = (0, 7)
+HALF_LAYERS = ((1, 2, 3), (4, 5, 6))
 
 
 def part(q):
-    return slice(q * W, (q + 1) * W)
+    return slice(q * 256, (q + 1) * 256)
 
 
 def kernel(
@@ -122,8 +121,8 @@
     jumps,
     pre,
     bpre,
-    ends_v,
-    moved_v,
+    edge_out,
+    edge_in,
     folded_v,
     resid,
     direc,
@@ -230,10 +229,6 @@
                     device_id_type=MESH,
                 ).start()
 
-    pl.semaphore_wait(barrier, len(tm_near) + len(space_near))
-    send_end(0, 0, init_v, pl.ds(0, CUT))
-    send_end(0, 4, init_v, pl.ds(CUT, E - CUT))
-
     row, col = iota((R, R), 0), iota((R, R), 1)
     to_face = one_hot(col == (row & 31) * 6 + (row >> 5))
     lower = send_v[0:1, :] & (E - 1)
@@ -263,6 +258,25 @@
     rim_out[0, 1] = rim[0:FD, 0:NB]
     rim_out[0, 0] = rim[FD : 2 * FD, NB : 2 * NB]
 
+    for k in SIDE_LAYERS:
+        place[:, layer(k)] = one_hot(column_ids == slots[k])
+    for n, c in enumerate(SIDES):
+        edge_out[n] = dot(xs[H:D, :], place[:, c]) + dot(xs[D + H : 2 * D, :], place[:, c])
+
+    pl.semaphore_wait(barrier, len(tm_near) + len(space_near))
+
+    @pl.when(t < nt - 1)
+    def _():
+        pltpu.make_async_remote_copy(
+            src_ref=edge_out,
+            dst_ref=edge_in,
+            send_sem=end_send.at[1],
+            recv_sem=end_recv.at[4],
+            device_id=up,
+            device_id_type=MESH,
+        ).start()
+
+    send_end(0, 0, init_v, pl.ds(0, E))
     send_rims(0)
     know("tm", 0)
     know("space", 0)
@@ -299,7 +313,7 @@
     xs[2 * D : 2 * D + 16, :] = jnp.concatenate([ch, cm, cl, jnp.zeros((13, E), BF16)], axis=0)
     for q in range(4):
         c = part(q)
-        for k in (2 * q, 2 * q + 1):
+        for k in {2 * q, 2 * q + 1} - set(SIDE_LAYERS):
             place[:, layer(k)] = one_hot(column_ids == slots[k])
         moved = dot(xs[...], place[:, c])
         coef_v[:, c] = moved[2 * D : 2 * D + 1] + moved[2 * D + 1 : 2 * D + 2] + moved[2 * D + 2 : 2 * D + 3]
@@ -406,29 +420,16 @@
 
     know("tm", 1)
     know("space", 1)
-    def take_ends(first, last):
-        eh, el = split(end_in[0, :, first:last])
-        ends_v[0:H, first:last] = eh
-        ends_v[H : 2 * H, first:last] = el
-
-    end_arrived(end_in.at[0, :, pl.ds(0, CUT)], 0)
-    take_ends(0, CUT)
-    for c in SIDES:
-        moved_v[:, c] = dot(ends_v[:, 0:CUT], place[0:CUT, c])
-    end_arrived(end_in.at[0, :, pl.ds(CUT, E - CUT)], 4)
-    take_ends(CUT, E)
-    for c in SIDES:
-        moved_v[:, c] = moved_v[:, c] + dot(ends_v[:, CUT:E], place[CUT:E, c])
-
-    def slab_start(c):
-        moved = moved_v[:, c]
-        jump = start_v[:, c] - jnp.where(t == 0, 0.0, moved[:H] + moved[H:])
+    end_arrived(edge_in, 4)
+
+    def slab_start(c, before):
+        jump = start_v[:, c] - jnp.where(t == 0, 0.0, before)
         jumps[0, R:, c] = jump
         t3[:, c] = stack3(jump)
         direc[:, c] = bpre[:, c] - dot(w_both[...], t3[:, c]) * inverse_coef[:, c]
 
-    for c in SIDES:
-        slab_start(c)
+    for n, c in enumerate(SIDES):
+        slab_start(c, edge_in[n])
     rims_arrived(0)
     for _, c, _, added in rim_terms(0):
         pre[:, c] = pre[:, c] - added[:D]
@@ -442,19 +443,22 @@
     turned = dot(jnp.concatenate(split(rim), axis=0), out_map)
     rim_out[1, 0] = turned[:FD] + turned[FD:]
     send_rims(1)
-    lateral_jumps(0, MIDDLE_LAYERS)
-    move_rhs(MIDDLE)
-    start_residual(MIDDLE)
-    moved_v[:, MIDDLE] = dot(ends_v[...], place[:, MIDDLE])
-    slab_start(MIDDLE)
-    x3[:, MIDDLE] = stack3(direc[:, MIDDLE])
-    send_end(1, 3, direc, pl.ds(W, E - 2 * W))
+    for n, c in enumerate(HALVES):
+        lateral_jumps(0, HALF_LAYERS[n])
+        move_rhs(c)
+        start_residual(c)
+        if n == 0:
+            end_arrived(end_in.at[0], 0)
+        moved = dot(jnp.concatenate(split(end_in[0]), axis=0), place[:, c])
+        slab_start(c, moved[:H] + moved[H:])
+        send_end(1, 3 + 2 * n, direc, pl.ds(c.start, c.stop - c.start))
+        x3[:, c] = stack3(direc[:, c])
     know("space", 2)
 
     work[...] = dot(w_vol[...], x3[...])
     residual = pre[...] - dot(w_time[...], t3[...])
     resid[...] = residual
-    lateral_jumps(1, SIDE_LAYERS + MIDDLE_LAYERS)
+    lateral_jumps(1, range(LAYERS))
     without_rims(1)
     pre[...] = apply_local(1, slice(0, E))
     j0, j1 = jumps[0, :R], jumps[1, :R]
@@ -481,8 +485,10 @@
         return sum(found[:, layer(k)] for k in range((c.stop - c.start) // NB))
 
     def middle_sums():
-        end_arrived(end_in.at[1, :, pl.ds(W, E - 2 * W)], 3)
-        folded_v[...] = image_sums(MIDDLE)
+        for n, c in enumerate(HALVES):
+            end_arrived(end_in.at[1, :, pl.ds(c.start, c.stop - c.start)], 3 + 2 * n)
+            found = image_sums(c)
+            folded_v[...] = folded_v[...] + found if n else found
 
     rims_last = lax.rem(p, LAYERS) == 0
 
@@ -553,6 +559,7 @@
     @pl.when(t < nt - 1)
     def _():
         arrived(end_in, end_send.at[0])
+        arrived(edge_in, end_send.at[1])
 
     for side, there in ((0, p < ns - 1), (1, p > 0)):
 
@@ -617,8 +624,8 @@
             vmem((2, 256, E), F32),
             vmem((D, E), F32),
             vmem((D, E), F32),
-            vmem((2 * H, E), BF16),
-            vmem((2 * H, E), F32),
+            vmem((2, H, NB), F32),
+            vmem((2, H, NB), F32),
             vmem((8, NB), F32),
             vmem((D, E), F32),
             vmem((D, E), F32),
@@ -635,8 +642,8 @@
             vmem((nt, 1, NB), F32),
             vmem((nt + ns, 1, NB), F32),
             dma((6,)),
-            dma((1,)),
-            dma((5,)),
+            dma((2,)),
+            dma((6,)),
             dma((2,)),
             dma((2, 2)),
             dma((1,)),

time: 35.4 us -> 35 us (0.989)
  Pallas kernels: 34.7 us -> 34.2 us
    pallas_call x1, Pallas kernels: 33.6 us -> 33.1 us  [on_device(): pl.pallas_call(functools.partial(kernel, nt, ns), out_shape=(jax.ShapeDty...]
where the time goes in v6:
time: 35 us; the launch traced here: 34.8 us
  Pallas kernels  34.2 us (98%)
  between operations  0.64 us (2%)
    pallas_call x1, Pallas kernels, on_device(): pl.pallas_call(functools.partial(kernel, nt, ns), out_shape=(jax.ShapeDty...  33.1 us
    pallas_call x1, Pallas kernels, on_device(): pl.pallas_call(functools.partial(finish, float(E * nt * ns)), out_shape=(...  1.08 us

profile of v6, /device:TPU:1, one launch (start us, length us, event | category | flops | bytes accessed | tf_op | source)
XLA Modules:
  0.0 34.8 jit_solution(10333306193848083065)
XLA Ops:
  0.6 33.1 %shard_map.130 = (f32[128,1024]{1,0:T(8,128)S(1)}, f32[128,1024]{1,0:T(8,128)S(1)}, f32[8,1024]{1,0:T(8,128)S(1)}, f32[1,128]{1,0:T(1,128)S(1)}) custom-call(f32[1,128,1024]{2,1,0:T(8,128)} %init_h.1, f32[1,128,1024]{2,1,0:T(8,128)} %rhs_h.1, f32[1,1024]{1,0:T(1,128)} %bitcast.8, f32[128,128]{1,0:T(8,128)} %stiff_h.1, f32[128,128]{1,0:T(8,128)} %binv_h.1, ...), custom_call_target="tpu_custom_call" | custom-call | flops 4000000000 | bytes 3145728 | tf_op jit(solution)/shard_map/pallas_call | solution.py:601
  33.8 1.1 %shard_map.131 = (f32[1,128,1024]{2,1,0:T(8,128)}, f32[1,1024]{1,0:T(1,128)}, f32[1,128]{1,0:T(1,128)}) custom-call(f32[128,1024]{1,0:T(8,128)S(1)} %get-tuple-element.10.init_v, f32[128,1024]{1,0:T(8,128)S(1)} %get-tuple-element.11.dir_v, f32[8,1024]{1,0:T(8,128)S(1)} %get-tuple-element.12.eta_v, f32[1,128]{1,0:T(1,128)S(1)} %get-tuple-element.13.tot_v), custom_call_target="tpu_custom_call" | custom-call | flops 300000 | bytes 1048576 | tf_op jit(solution)/shard_map/pallas_call | solution.py:673

commit v7 on v6

--- a/solution.py
+++ b/solution.py
@@ -123,7 +123,6 @@
     bpre,
     edge_out,
     edge_in,
-    folded_v,
     resid,
     direc,
     rows,
@@ -484,18 +483,6 @@
         rows[:, c] = found
         return sum(found[:, layer(k)] for k in range((c.stop - c.start) // NB))
 
-    def middle_sums():
-        for n, c in enumerate(HALVES):
-            end_arrived(end_in.at[1, :, pl.ds(c.start, c.stop - c.start)], 3 + 2 * n)
-            found = image_sums(c)
-            folded_v[...] = folded_v[...] + found if n else found
-
-    rims_last = lax.rem(p, LAYERS) == 0
-
-    @pl.when(rims_last)
-    def _():
-        middle_sums()
-
     for n, c in enumerate(SIDES):
         end_arrived(end_in.at[1, :, pl.ds(c.start, W)], 1 + n)
     rims_arrived(1)
@@ -506,11 +493,9 @@
 
     folded = image_sums(SIDES[0]) + image_sums(SIDES[1])
 
-    @pl.when(jnp.logical_not(rims_last))
-    def _():
-        middle_sums()
-
-    folded = folded + folded_v[...]
+    for n, c in enumerate(HALVES):
+        end_arrived(end_in.at[1, :, pl.ds(c.start, c.stop - c.start)], 3 + 2 * n)
+        folded = folded + image_sums(c)
     sums = jnp.sum(folded, axis=1, keepdims=True)
     diagonal = iota((8, NB), 0) == iota((8, NB), 1)
     message = jnp.sum(jnp.where(diagonal, sums, 0.0), axis=0, keepdims=True)
@@ -626,7 +611,6 @@
             vmem((D, E), F32),
             vmem((2, H, NB), F32),
             vmem((2, H, NB), F32),
-            vmem((8, NB), F32),
             vmem((D, E), F32),
             vmem((D, E), F32),
             vmem((8, E), F32),

time: 35 us -> 35 us (level)
  no operation moved by 1% of the time
where the time goes in v7:
time: 35 us; the launch traced here: 34.8 us
  Pallas kernels  34.2 us (98%)
  between operations  0.64 us (2%)
    pallas_call x1, Pallas kernels, on_device(): pl.pallas_call(functools.partial(kernel, nt, ns), out_shape=(jax.ShapeDty...  33.1 us
    pallas_call x1, Pallas kernels, on_device(): pl.pallas_call(functools.partial(finish, float(E * nt * ns)), out_shape=(...  1.08 us

profile of v7, /device:TPU:1, one launch (start us, length us, event | category | flops | bytes accessed | tf_op | source)
XLA Modules:
  0.0 34.8 jit_solution(1550764451264878425)
XLA Ops:
  0.6 33.1 %shard_map.130 = (f32[128,1024]{1,0:T(8,128)S(1)}, f32[128,1024]{1,0:T(8,128)S(1)}, f32[8,1024]{1,0:T(8,128)S(1)}, f32[1,128]{1,0:T(1,128)S(1)}) custom-call(f32[1,128,1024]{2,1,0:T(8,128)} %init_h.1, f32[1,128,1024]{2,1,0:T(8,128)} %rhs_h.1, f32[1,1024]{1,0:T(1,128)} %bitcast.8, f32[128,128]{1,0:T(8,128)} %stiff_h.1, f32[128,128]{1,0:T(8,128)} %binv_h.1, ...), custom_call_target="tpu_custom_call" | custom-call | flops 4000000000 | bytes 3145728 | tf_op jit(solution)/shard_map/pallas_call | solution.py:586
  33.8 1.1 %shard_map.131 = (f32[1,128,1024]{2,1,0:T(8,128)}, f32[1,1024]{1,0:T(1,128)}, f32[1,128]{1,0:T(1,128)}) custom-call(f32[128,1024]{1,0:T(8,128)S(1)} %get-tuple-element.10.init_v, f32[128,1024]{1,0:T(8,128)S(1)} %get-tuple-element.11.dir_v, f32[8,1024]{1,0:T(8,128)S(1)} %get-tuple-element.12.eta_v, f32[1,128]{1,0:T(1,128)S(1)} %get-tuple-element.13.tot_v), custom_call_target="tpu_custom_call" | custom-call | flops 300000 | bytes 1048576 | tf_op jit(solution)/shard_map/pallas_call | solution.py:657
